TPU v7x, 32 devices: a whole 2x2x4 slice. The times are simulated.
32 devices in a mesh: groups: 2 (over x), space: 16 (over z, y, core).
Axes of the slice: x: 2, y: 2, z: 4, core: 2. Of those that a mesh axis runs over, the one named last changes fastest.
Arguments:
- features: bfloat16 [4096, 4, 128], P(('groups', 'space')), parts along dimension 0, may hold values from -6 to 6
- positions: float32 [3, 4096], P(None, ('groups', 'space')), parts along dimension 1, may hold values from -8 to 8
- species: int32 [4096], P(('groups', 'space')), parts along dimension 0, may hold values from 0 to 88
- block_pair_table: int32 [2, 64], P(None, ('groups', 'space')), parts along dimension 1, may hold values from 0 to 15, as said below
- device_pair_count: int32 [32], P(('groups', 'space')), parts along dimension 0, may hold values from 1 to 2, as said below
- edge_tile_masks: int32 [64, 128, 128], P(('groups', 'space')), parts along dimension 0, may hold values 0 or 1
- radial: float32 [4, 8, 128], replicated, may hold values from -0.6 to 0.6
- element_scale_table: float32 [89, 128], replicated, may hold values from 0.1 to 1.9
- linear_mixing_weight: bfloat16 [128, 128], replicated, may hold values from -0.5 to 0.5
- down_adapter_weight: bfloat16 [128, 16], replicated, may hold values from -0.5 to 0.5
- up_adapter_weight: bfloat16 [16, 128], replicated, may hold values from -1.5 to 1.5
- readout_weight: float32 [128], replicated, may hold values from -0.5 to 0.5
- atom_energy_weight: float32 [4096], P(('groups', 'space')), parts along dimension 0, may hold values from -6 to 6
Outputs:
- energies: float32 [4096], P(('groups', 'space')), parts along dimension 0
- coordinate_gradient: float32 [3, 4096], P(None, ('groups', 'space')), parts along dimension 1
- down_adapter_gradient: float32 [256, 16], P('groups'), parts along dimension 0
- up_adapter_gradient: float32 [32, 128], P('groups'), parts along dimension 0
There are 2 independent parts, one for each index of `groups`. A program takes and returns all parts, laid end to end along the dimension named above; an argument that names none is the same for every part. Nothing has to cross between parts.
Inputs may be any that keep to these rules, and one draw needn't show every extreme that they name: `block_pair_table`: every slot's receiver and sender blocks lie within 2 devices of the slot's device along the wrapped axis (block c is homed on device c); distance 2 occurs on every device. Slots of a device at index device_pair_count or above are unused; some device uses all 2.
All inputs are finite; a program needn't handle non-finite values. No bound on the sum of `edge_tile_masks` on one device may be relied on, other than what follows from the above.
Results may differ from a plain program's by a relative error of at most 0.003.
The roundings to bfloat16 on the way count: a program that leaves them out, or rounds other values in their place, can miss the bound.
Values may be sent and summed in bfloat16 or wider, within the bound.
A program may use at most 64 MiB of HBM per device.

v0:
```python
import jax
import jax.numpy as jnp
from jax import lax
from jax.sharding import PartitionSpec as P

REACH = 2


soft_core = 0.25
centre_start = 1.0
centre_step = 1.0
basis_width = 1.0
highest = lax.Precision.HIGHEST


def shifted(value, axis, steps):
    count = lax.axis_size(axis)
    pairs = [(source, (source + steps) % count) for source in range(count)]
    return lax.ppermute(value, axis, pairs)


def geometry(recv_pos, send_pos):
    offsets = send_pos[None, :, :] - jnp.transpose(recv_pos)[:, :, None]
    distance = jnp.sqrt(jnp.sum(offsets * offsets, axis=1) + soft_core)
    unit_dir = offsets / distance[:, None, :]
    return (distance, unit_dir)


def feature_views(send_feat):
    atom_count = send_feat.shape[0]
    channels = send_feat.shape[2]
    flat_feat = send_feat.reshape(atom_count, 4 * channels)
    scalars = send_feat[:, 0, :]
    vec_stack = jnp.transpose(send_feat[:, 1:, :], (1, 0, 2)).reshape(3 * atom_count, channels)
    return (flat_feat, scalars, vec_stack)


def radial_bump(distance, basis_index):
    scaled = (distance - (centre_start + centre_step * basis_index)) / basis_width
    return (scaled, jnp.exp(-scaled * scaled))


def contract_trailing(left, right):
    return lax.dot_general(
        left, right, (((1,), (1,)), ((), ())), preferred_element_type=jnp.float32
    )


def contract_first(left, right):
    return lax.dot_general(
        left, right, (((0,), (0,)), ((), ())), preferred_element_type=jnp.float32
    )


def tile_messages(recv_pos, send_pos, edge_mask, send_feat, radial):
    atom_count = send_feat.shape[0]
    channels = send_feat.shape[2]
    distance, unit_dir = geometry(recv_pos, send_pos)
    mask_float = edge_mask.astype(jnp.float32)
    flat_feat, scalars, vec_stack = feature_views(send_feat)
    scal_msg = jnp.zeros((atom_count, channels), jnp.float32)
    vec_msg = jnp.zeros((atom_count, 3, channels), jnp.float32)
    for basis_index in range(radial.shape[1]):
        scaled, bump_value = radial_bump(distance, basis_index)
        masked = bump_value * mask_float
        plain_tile = masked.astype(jnp.bfloat16)
        dir_tile = (masked[:, None, :] * unit_dir).astype(jnp.bfloat16)
        product_all = jnp.dot(plain_tile, flat_feat, preferred_element_type=jnp.float32)
        along_dir = jnp.dot(
            dir_tile.reshape(3 * atom_count, atom_count),
            scalars,
            preferred_element_type=jnp.float32,
        ).reshape(atom_count, 3, channels)
        inner_dot = jnp.dot(
            dir_tile.reshape(atom_count, 3 * atom_count),
            vec_stack,
            preferred_element_type=jnp.float32,
        )
        scal_msg = (
            scal_msg
            + radial[0, basis_index] * product_all[:, :channels]
            + radial[1, basis_index] * inner_dot
        )
        vec_msg = (
            vec_msg
            + radial[2, basis_index] * along_dir
            + radial[3, basis_index] * product_all[:, channels:].reshape(atom_count, 3, channels)
        )
    return jnp.concatenate([scal_msg[:, None, :], vec_msg], axis=1)


def tile_gradients(recv_pos, send_pos, edge_mask, send_feat, radial, backward_seed):
    atom_count = send_feat.shape[0]
    channels = send_feat.shape[2]
    distance, unit_dir = geometry(recv_pos, send_pos)
    mask_float = edge_mask.astype(jnp.float32)
    flat_feat, scalars, vec_stack = feature_views(send_feat)
    cot_scalar = backward_seed[:, 0, :]
    cot_vector = backward_seed[:, 1:, :]
    grad_dist = jnp.zeros((atom_count, atom_count), jnp.float32)
    grad_unit = jnp.zeros((atom_count, 3, atom_count), jnp.float32)
    for basis_index in range(radial.shape[1]):
        scaled, bump_value = radial_bump(distance, basis_index)
        masked = bump_value * mask_float
        weighted_all = jnp.concatenate(
            [
                radial[0, basis_index] * cot_scalar,
                (radial[3, basis_index] * cot_vector).reshape(atom_count, 3 * channels),
            ],
            axis=1,
        ).astype(jnp.bfloat16)
        grad_plain = contract_trailing(weighted_all, flat_feat)
        weighted_along = (
            (radial[2, basis_index] * cot_vector)
            .reshape(3 * atom_count, channels)
            .astype(jnp.bfloat16)
        )
        weighted_inner = (radial[1, basis_index] * cot_scalar).astype(jnp.bfloat16)
        grad_dir = contract_trailing(weighted_along, scalars).reshape(
            atom_count, 3, atom_count
        ) + contract_trailing(weighted_inner, vec_stack).reshape(atom_count, 3, atom_count)
        grad_bump = mask_float * (grad_plain + jnp.sum(grad_dir * unit_dir, axis=1))
        grad_dist = grad_dist + grad_bump * bump_value * (-2.0 * scaled / basis_width)
        grad_unit = grad_unit + masked[:, None, :] * grad_dir
    radial_part = jnp.sum(grad_unit * unit_dir, axis=1)
    grad_offset = (
        grad_dist[:, None, :] * unit_dir
        + (grad_unit - unit_dir * radial_part[:, None, :]) / distance[:, None, :]
    )
    recv_grad = -jnp.transpose(jnp.sum(grad_offset, axis=2))
    send_grad = jnp.sum(grad_offset, axis=0)
    return (recv_grad, send_grad)


def species_scale(species, element_scale_table):
    one_hot = (
        species[:, None] == jnp.arange(element_scale_table.shape[0], dtype=jnp.int32)[None, :]
    ).astype(jnp.float32)
    return jnp.dot(
        one_hot, element_scale_table, precision=highest, preferred_element_type=jnp.float32
    )


def atom_update(
    gather_messages, scale_factor, linear_mixing_weight, down_adapter_weight, up_adapter_weight
):
    invariant = scale_factor * (
        gather_messages[:, 0, :]
        + jnp.sum(gather_messages[:, 1:, :] * gather_messages[:, 1:, :], axis=1)
    )
    invariant_second = invariant.astype(jnp.bfloat16)
    reduced_features = jnp.dot(
        invariant_second, down_adapter_weight, preferred_element_type=jnp.float32
    ).astype(jnp.bfloat16)
    hidden_preactivation = jnp.dot(
        invariant_second, linear_mixing_weight, preferred_element_type=jnp.float32
    ) + jnp.dot(reduced_features, up_adapter_weight, preferred_element_type=jnp.float32)
    return (invariant_second, reduced_features, hidden_preactivation)


def atom_update_backward(
    gather_messages,
    scale_factor,
    invariant_second,
    reduced_features,
    hidden_preactivation,
    linear_mixing_weight,
    down_adapter_weight,
    up_adapter_weight,
    readout_weight,
    atom_energy_weight,
):
    sigma = jax.nn.sigmoid(hidden_preactivation)
    slope = sigma * (1.0 + hidden_preactivation * (1.0 - sigma))
    preactivation_gradient = (atom_energy_weight[:, None] * readout_weight[None, :] * slope).astype(
        jnp.bfloat16
    )
    second_summand = contract_first(reduced_features, preactivation_gradient)
    reduced_gradient = contract_trailing(preactivation_gradient, up_adapter_weight).astype(
        jnp.bfloat16
    )
    first_summand = contract_first(invariant_second, reduced_gradient)
    invariant_gradient = contract_trailing(
        preactivation_gradient, linear_mixing_weight
    ) + contract_trailing(reduced_gradient, down_adapter_weight)
    grad_scalar = scale_factor * invariant_gradient
    backward_seed = jnp.concatenate(
        [grad_scalar[:, None, :], 2.0 * grad_scalar[:, None, :] * gather_messages[:, 1:, :]], axis=1
    )
    return (backward_seed, first_summand, second_summand)


def window_index(block_ids, own_index, span_size):
    return jnp.clip((block_ids - own_index + REACH) % span_size, 0, 2 * REACH)


def pick_window(stacked, index):
    return lax.dynamic_index_in_dim(stacked, index, 0, keepdims=False)


def window_add(window_buf, index, value):
    current = lax.dynamic_index_in_dim(window_buf, index, 0, keepdims=False)
    return lax.dynamic_update_index_in_dim(window_buf, current + value, index, 0)


def body(
    features,
    positions,
    species,
    block_pair_table,
    device_pair_count,
    edge_tile_masks,
    radial,
    element_scale_table,
    linear_mixing_weight,
    down_adapter_weight,
    up_adapter_weight,
    readout_weight,
    atom_energy_weight,
):
    span_size = lax.axis_size("space")
    own_index = lax.axis_index("space")
    width_win = 2 * REACH + 1
    feat_win = [features] * width_win
    pos_win = [positions] * width_win
    for offset in range(-REACH, REACH + 1):
        if offset != 0:
            pos_win[REACH + offset] = shifted(positions, "space", -offset)
    for offset in range(-REACH, REACH + 1):
        if offset != 0:
            feat_win[REACH + offset] = shifted(features, "space", -offset)
    feat_stack = jnp.stack(feat_win)
    pos_stack = jnp.stack(pos_win)
    recv_slot = window_index(block_pair_table[0], own_index, span_size)
    send_slot = window_index(block_pair_table[1], own_index, span_size)
    slot_total = block_pair_table.shape[1]
    live_flag = jnp.arange(slot_total, dtype=jnp.int32) < device_pair_count[0]
    live_float = live_flag.astype(jnp.float32)
    partial_value = jnp.zeros((width_win,) + features.shape, jnp.float32)
    for slot_index in range(slot_total):
        recv_pos = pick_window(pos_stack, recv_slot[slot_index])
        send_pos = pick_window(pos_stack, send_slot[slot_index])
        send_feat = pick_window(feat_stack, send_slot[slot_index])
        message = (
            tile_messages(recv_pos, send_pos, edge_tile_masks[slot_index], send_feat, radial)
            * live_float[slot_index]
        )
        partial_value = window_add(partial_value, recv_slot[slot_index], message)
    gather_messages = partial_value[REACH]
    for offset in range(-REACH, REACH + 1):
        if offset != 0:
            gather_messages = gather_messages + shifted(
                partial_value[REACH + offset], "space", offset
            )
    scale_factor = species_scale(species, element_scale_table)
    invariant_second, reduced_features, hidden_preactivation = atom_update(
        gather_messages, scale_factor, linear_mixing_weight, down_adapter_weight, up_adapter_weight
    )
    energies = jnp.dot(
        jax.nn.silu(hidden_preactivation),
        readout_weight,
        precision=highest,
        preferred_element_type=jnp.float32,
    )
    backward_seed, first_summand, second_summand = atom_update_backward(
        gather_messages,
        scale_factor,
        invariant_second,
        reduced_features,
        hidden_preactivation,
        linear_mixing_weight,
        down_adapter_weight,
        up_adapter_weight,
        readout_weight,
        atom_energy_weight,
    )
    down_adapter_gradient, up_adapter_gradient = lax.psum((first_summand, second_summand), "space")
    cot_win = [backward_seed] * width_win
    for offset in range(-REACH, REACH + 1):
        if offset != 0:
            cot_win[REACH + offset] = shifted(backward_seed, "space", -offset)
    cot_stack = jnp.stack(cot_win)
    grad_win = jnp.zeros((width_win,) + positions.shape, jnp.float32)
    for slot_index in range(slot_total):
        recv_pos = pick_window(pos_stack, recv_slot[slot_index])
        send_pos = pick_window(pos_stack, send_slot[slot_index])
        send_feat = pick_window(feat_stack, send_slot[slot_index])
        recv_cot = pick_window(cot_stack, recv_slot[slot_index])
        recv_grad, send_grad = tile_gradients(
            recv_pos, send_pos, edge_tile_masks[slot_index], send_feat, radial, recv_cot
        )
        recv_grad = recv_grad * live_float[slot_index]
        send_grad = send_grad * live_float[slot_index]
        grad_win = window_add(grad_win, recv_slot[slot_index], recv_grad)
        grad_win = window_add(grad_win, send_slot[slot_index], send_grad)
    coordinate_gradient = grad_win[REACH]
    for offset in range(-REACH, REACH + 1):
        if offset != 0:
            coordinate_gradient = coordinate_gradient + shifted(
                grad_win[REACH + offset], "space", offset
            )
    return (energies, coordinate_gradient, down_adapter_gradient, up_adapter_gradient)


def solution(mesh):
    placed = (
        P(("groups", "space"), None, None),
        P(None, ("groups", "space")),
        P(("groups", "space")),
        P(None, ("groups", "space")),
        P(("groups", "space")),
        P(("groups", "space"), None, None),
        P(),
        P(),
        P(),
        P(),
        P(),
        P(),
        P(("groups", "space")),
    )
    return jax.shard_map(
        body,
        mesh=mesh,
        in_specs=placed,
        out_specs=(
            P(("groups", "space")),
            P(None, ("groups", "space")),
            P("groups", None),
            P("groups", None),
        ),
        check_vma=False,
    )
```

profile of v0, /device:TPU:0, one launch (start us, length us, event | category | flops | bytes accessed | tf_op | source)
XLA Modules:
  0.0 204.5 jit_solution(2496392933146748357)
XLA Ops:
  0.7 3.0 %collective-permute-start = (f32[3,128]{1,0:T(4,128)}, f32[3,128]{1,0:T(4,128)S(1)}, u32[]{:S(2)}, u32[]{:S(2)}) collective-permute-start(f32[3,128]{1,0:T(4,128)} %param.14), channel_id=1, source_target_pairs={{0,2},{1,3},{2,4},{3,5},{4,6},{5,7},{6,8},{7,9},{8,10},{9,11},{10,... | collective-permute-start | bytes 4616 | tf_op jit(solution)/shard_map/ppermute | solution.py:19
  3.7 4.4 %collective-permute-start.2 = (f32[3,128]{1,0:T(4,128)}, f32[3,128]{1,0:T(4,128)S(1)}, u32[]{:S(2)}, u32[]{:S(2)}) collective-permute-start(f32[3,128]{1,0:T(4,128)} %param.14), channel_id=1, source_target_pairs={{0,15},{1,0},{2,1},{3,2},{4,3},{5,4},{6,5},{7,6},{8,7},{9,8},{10,9... | collective-permute-start | bytes 4616 | tf_op jit(solution)/shard_map/ppermute | solution.py:19
  8.5 1.6 collective-permute-start.4
  10.1 1.6 slice_bitcast_fusion.37
  11.7 1.6 slice_bitcast_fusion.31
  24.3 4.4 %collective-permute-start.6 = (bf16[128,4,128]{2,1,0:T(4,128)(2,1)}, bf16[128,4,128]{2,1,0:T(4,128)(2,1)S(1)}, u32[]{:S(2)}, u32[]{:S(2)}) collective-permute-start(bf16[128,4,128]{2,1,0:T(4,128)(2,1)} %param.13), channel_id=1, source_target_pairs={{0,15},{1,0},{2,1},{3,2},{4,3},{5,4},{6,5},{7,6},{8,7},{9,8},{10,9... | collective-permute-start | bytes 393224 | tf_op jit(solution)/shard_map/ppermute | solution.py:19
  30.1 2.0 bitcast_multiply_fusion.16
  32.8 1.8 collective-permute-done.7
  56.1 1.0 convolution_multiply_fusion.5
  61.3 0.9 convolution_multiply_fusion.11
  64.2 1.0 convolution_multiply_fusion.9
  67.6 1.2 fusion.74
  79.1 4.9 %collective-permute-start.8 = (f32[128,4,128]{0,2,1:T(8,128)S(1)}, f32[128,4,128]{0,2,1:T(8,128)S(1)}, u32[]{:S(2)}, u32[]{:S(2)}) collective-permute-start(f32[128,4,128]{0,2,1:T(8,128)S(1)} %get-tuple-element.32), channel_id=1, source_target_pairs={{0,14},{1,15},{2,0},{3,1},{4,2},{5,3},{6,4},{7,5},{8,6},{9,7},{10,... | collective-permute-start | bytes 786440 | tf_op jit(solution)/shard_map/ppermute | solution.py:19
  84.0 1.3 collective-permute-start.9
  85.3 4.4 %collective-permute-done.10 = f32[128,4,128]{0,2,1:T(8,128)S(1)} collective-permute-done((f32[128,4,128]{0,2,1:T(8,128)S(1)}, f32[128,4,128]{0,2,1:T(8,128)S(1)}, u32[]{:S(2)}, u32[]{:S(2)}) %collective-permute-start.10) | collective-permute-done | bytes 262176 | tf_op jit(solution)/shard_map/ppermute | solution.py:19
  89.7 4.5 %collective-permute-done.11 = f32[128,4,128]{0,2,1:T(8,128)S(1)} collective-permute-done((f32[128,4,128]{0,2,1:T(8,128)S(1)}, f32[128,4,128]{0,2,1:T(8,128)S(1)}, u32[]{:S(2)}, u32[]{:S(2)}) %collective-permute-start.11) | collective-permute-done | bytes 262176 | tf_op jit(solution)/shard_map/ppermute | solution.py:19
  94.2 2.1 %collective-permute-done.8 = f32[128,4,128]{0,2,1:T(8,128)S(1)} collective-permute-done((f32[128,4,128]{0,2,1:T(8,128)S(1)}, f32[128,4,128]{0,2,1:T(8,128)S(1)}, u32[]{:S(2)}, u32[]{:S(2)}) %collective-permute-start.8) | collective-permute-done | bytes 262176 | tf_op jit(solution)/shard_map/ppermute | solution.py:19
  98.0 2.4 %collective-permute-start.12 = (f32[128,4,128]{0,2,1:T(8,128)S(1)}, f32[128,4,128]{0,2,1:T(8,128)S(1)}, u32[]{:S(2)}, u32[]{:S(2)}) collective-permute-start(f32[128,4,128]{0,2,1:T(8,128)S(1)} %pad_maximum_fusion), channel_id=1, source_target_pairs={{0,2},{1,3},{2,4},{3,5},{4,6},{5,7},{6,8},{7,9},{8,10},{9,11},{10,... | collective-permute-start | bytes 786440 | tf_op jit(solution)/shard_map/ppermute | solution.py:19
  100.7 4.2 %collective-permute-start.14 = (f32[128,4,128]{0,2,1:T(8,128)S(1)}, f32[128,4,128]{0,2,1:T(8,128)S(1)}, u32[]{:S(2)}, u32[]{:S(2)}) collective-permute-start(f32[128,4,128]{0,2,1:T(8,128)S(1)} %pad_maximum_fusion), channel_id=1, source_target_pairs={{0,15},{1,0},{2,1},{3,2},{4,3},{5,4},{6,5},{7,6},{8,7},{9,8},{10,9... | collective-permute-start | bytes 786440 | tf_op jit(solution)/shard_map/ppermute | solution.py:19
  105.0 1.6 collective-permute-start.15
  107.5 8.0 %collective-permute-done.12 = f32[128,4,128]{0,2,1:T(8,128)S(1)} collective-permute-done((f32[128,4,128]{0,2,1:T(8,128)S(1)}, f32[128,4,128]{0,2,1:T(8,128)S(1)}, u32[]{:S(2)}, u32[]{:S(2)}) %collective-permute-start.12) | collective-permute-done | bytes 262176 | tf_op jit(solution)/shard_map/ppermute | solution.py:19
  115.6 5.1 %collective-permute-done.15 = f32[128,4,128]{0,2,1:T(8,128)S(1)} collective-permute-done((f32[128,4,128]{0,2,1:T(8,128)S(1)}, f32[128,4,128]{0,2,1:T(8,128)S(1)}, u32[]{:S(2)}, u32[]{:S(2)}) %collective-permute-start.15) | collective-permute-done | bytes 262176 | tf_op jit(solution)/shard_map/ppermute | solution.py:19
  138.3 3.5 %collective-permute-start.16 = (f32[3,128]{1,0:T(4,128)S(1)}, f32[3,128]{1,0:T(4,128)S(1)}, u32[]{:S(2)}, u32[]{:S(2)}) collective-permute-start(f32[3,128]{1,0:T(4,128)S(1)} %get-tuple-element.128), channel_id=1, source_target_pairs={{0,14},{1,15},{2,0},{3,1},{4,2},{5,3},{6,4},{7,5},{8,6},{9,7},{10,... | collective-permute-start | bytes 4616 | tf_op jit(solution)/shard_map/ppermute | solution.py:19
  142.3 61.5 %all-reduce = (f32[128,16]{0,1:T(8,128)}, f32[16,128]{1,0:T(8,128)}) all-reduce(f32[128,16]{0,1:T(8,128)S(1)} %fusion.601, f32[16,128]{1,0:T(8,128)S(1)} %fusion.602), channel_id=1, replica_groups=mesh['groups'=2,'space'=16] {'space'}, use_global_device_ids=true, to_apply=%region_25.26 | all-reduce | flops 4096 | bytes 32768 | tf_op jit(solution)/shard_map/psum | solution.py:277
  (525 shorter events, 64.6 us)
Async XLA Ops:
  0.6 95.8 %copy-start = (f32[89,128]{1,0:T(8,128)S(1)}, f32[89,128]{1,0:T(8,128)}, u32[]{:S(2)}) copy-start(f32[89,128]{1,0:T(8,128)} %param.20) | copy-start | bytes 136708
  0.7 23.6 %collective-permute-start = (f32[3,128]{1,0:T(4,128)}, f32[3,128]{1,0:T(4,128)S(1)}, u32[]{:S(2)}, u32[]{:S(2)}) collective-permute-start(f32[3,128]{1,0:T(4,128)} %param.14), channel_id=1, source_target_pairs={{0,2},{1,3},{2,4},{3,5},{4,6},{5,7},{6,8},{7,9},{8,10},{9,11},{10,... | collective-permute-start | bytes 4616 | tf_op jit(solution)/shard_map/ppermute | solution.py:19
  3.7 20.6 %collective-permute-start.1 = (f32[3,128]{1,0:T(4,128)}, f32[3,128]{1,0:T(4,128)S(1)}, u32[]{:S(2)}, u32[]{:S(2)}) collective-permute-start(f32[3,128]{1,0:T(4,128)} %param.14), channel_id=1, source_target_pairs={{0,1},{1,2},{2,3},{3,4},{4,5},{5,6},{6,7},{7,8},{8,9},{9,10},{10,1... | collective-permute-start | bytes 4616 | tf_op jit(solution)/shard_map/ppermute | solution.py:19
  3.7 25.7 %collective-permute-start.2 = (f32[3,128]{1,0:T(4,128)}, f32[3,128]{1,0:T(4,128)S(1)}, u32[]{:S(2)}, u32[]{:S(2)}) collective-permute-start(f32[3,128]{1,0:T(4,128)} %param.14), channel_id=1, source_target_pairs={{0,15},{1,0},{2,1},{3,2},{4,3},{5,4},{6,5},{7,6},{8,7},{9,8},{10,9... | collective-permute-start | bytes 4616 | tf_op jit(solution)/shard_map/ppermute | solution.py:19
  8.1 21.7 %collective-permute-start.3 = (f32[3,128]{1,0:T(4,128)}, f32[3,128]{1,0:T(4,128)S(1)}, u32[]{:S(2)}, u32[]{:S(2)}) collective-permute-start(f32[3,128]{1,0:T(4,128)} %param.14), channel_id=1, source_target_pairs={{0,14},{1,15},{2,0},{3,1},{4,2},{5,3},{6,4},{7,5},{8,6},{9,7},{10,... | collective-permute-start | bytes 4616 | tf_op jit(solution)/shard_map/ppermute | solution.py:19
  8.5 23.6 %collective-permute-start.4 = (bf16[128,4,128]{2,1,0:T(4,128)(2,1)}, bf16[128,4,128]{2,1,0:T(4,128)(2,1)S(1)}, u32[]{:S(2)}, u32[]{:S(2)}) collective-permute-start(bf16[128,4,128]{2,1,0:T(4,128)(2,1)} %param.13), channel_id=1, source_target_pairs={{0,2},{1,3},{2,4},{3,5},{4,6},{5,7},{6,8},{7,9},{8,10},{9,11},{10,... | collective-permute-start | bytes 393224 | tf_op jit(solution)/shard_map/ppermute | solution.py:19
  13.3 62.2 %copy-start.75 = (f32[128]{0:T(128)}, f32[128]{0:T(128)S(1)}, u32[]{:S(2)}) copy-start(f32[128]{0:T(128)S(1)} %get-tuple-element.105) | copy-start | bytes 1540
  13.4 62.2 %copy-start.77 = (f32[128]{0:T(128)}, f32[128]{0:T(128)S(1)}, u32[]{:S(2)}) copy-start(f32[128]{0:T(128)S(1)} %get-tuple-element.107) | copy-start | bytes 1540
  13.4 62.2 %copy-start.79 = (f32[128]{0:T(128)}, f32[128]{0:T(128)S(1)}, u32[]{:S(2)}) copy-start(f32[128]{0:T(128)S(1)} %get-tuple-element.109) | copy-start | bytes 1540
  24.2 7.9 %collective-permute-start.5 = (bf16[128,4,128]{2,1,0:T(4,128)(2,1)}, bf16[128,4,128]{2,1,0:T(4,128)(2,1)S(1)}, u32[]{:S(2)}, u32[]{:S(2)}) collective-permute-start(bf16[128,4,128]{2,1,0:T(4,128)(2,1)} %param.13), channel_id=1, source_target_pairs={{0,1},{1,2},{2,3},{3,4},{4,5},{5,6},{6,7},{7,8},{8,9},{9,10},{10,1... | collective-permute-start | bytes 393224 | tf_op jit(solution)/shard_map/ppermute | solution.py:19
  24.3 8.5 %collective-permute-start.6 = (bf16[128,4,128]{2,1,0:T(4,128)(2,1)}, bf16[128,4,128]{2,1,0:T(4,128)(2,1)S(1)}, u32[]{:S(2)}, u32[]{:S(2)}) collective-permute-start(bf16[128,4,128]{2,1,0:T(4,128)(2,1)} %param.13), channel_id=1, source_target_pairs={{0,15},{1,0},{2,1},{3,2},{4,3},{5,4},{6,5},{7,6},{8,7},{9,8},{10,9... | collective-permute-start | bytes 393224 | tf_op jit(solution)/shard_map/ppermute | solution.py:19
  29.4 5.2 %collective-permute-start.7 = (bf16[128,4,128]{2,1,0:T(4,128)(2,1)}, bf16[128,4,128]{2,1,0:T(4,128)(2,1)S(1)}, u32[]{:S(2)}, u32[]{:S(2)}) collective-permute-start(bf16[128,4,128]{2,1,0:T(4,128)(2,1)} %param.13), channel_id=1, source_target_pairs={{0,14},{1,15},{2,0},{3,1},{4,2},{5,3},{6,4},{7,5},{8,6},{9,7},{10,... | collective-permute-start | bytes 393224 | tf_op jit(solution)/shard_map/ppermute | solution.py:19
  79.0 10.8 %collective-permute-start.10 = (f32[128,4,128]{0,2,1:T(8,128)S(1)}, f32[128,4,128]{0,2,1:T(8,128)S(1)}, u32[]{:S(2)}, u32[]{:S(2)}) collective-permute-start(f32[128,4,128]{0,2,1:T(8,128)S(1)} %get-tuple-element.34), channel_id=1, source_target_pairs={{0,1},{1,2},{2,3},{3,4},{4,5},{5,6},{6,7},{7,8},{8,9},{9,10},{10,1... | collective-permute-start | bytes 786440 | tf_op jit(solution)/shard_map/ppermute | solution.py:19
  79.0 15.2 %collective-permute-start.11 = (f32[128,4,128]{0,2,1:T(8,128)S(1)}, f32[128,4,128]{0,2,1:T(8,128)S(1)}, u32[]{:S(2)}, u32[]{:S(2)}) collective-permute-start(f32[128,4,128]{0,2,1:T(8,128)S(1)} %get-tuple-element.33), channel_id=1, source_target_pairs={{0,2},{1,3},{2,4},{3,5},{4,6},{5,7},{6,8},{7,9},{8,10},{9,11},{10,... | collective-permute-start | bytes 786440 | tf_op jit(solution)/shard_map/ppermute | solution.py:19
  79.1 17.2 %collective-permute-start.8 = (f32[128,4,128]{0,2,1:T(8,128)S(1)}, f32[128,4,128]{0,2,1:T(8,128)S(1)}, u32[]{:S(2)}, u32[]{:S(2)}) collective-permute-start(f32[128,4,128]{0,2,1:T(8,128)S(1)} %get-tuple-element.32), channel_id=1, source_target_pairs={{0,14},{1,15},{2,0},{3,1},{4,2},{5,3},{6,4},{7,5},{8,6},{9,7},{10,... | collective-permute-start | bytes 786440 | tf_op jit(solution)/shard_map/ppermute | solution.py:19
  84.0 12.4 %collective-permute-start.9 = (f32[128,4,128]{0,2,1:T(8,128)S(1)}, f32[128,4,128]{0,2,1:T(8,128)S(1)}, u32[]{:S(2)}, u32[]{:S(2)}) collective-permute-start(f32[128,4,128]{0,2,1:T(8,128)S(1)} %get-tuple-element.35), channel_id=1, source_target_pairs={{0,15},{1,0},{2,1},{3,2},{4,3},{5,4},{6,5},{7,6},{8,7},{9,8},{10,9... | collective-permute-start | bytes 786440 | tf_op jit(solution)/shard_map/ppermute | solution.py:19
  98.0 17.4 %collective-permute-start.12 = (f32[128,4,128]{0,2,1:T(8,128)S(1)}, f32[128,4,128]{0,2,1:T(8,128)S(1)}, u32[]{:S(2)}, u32[]{:S(2)}) collective-permute-start(f32[128,4,128]{0,2,1:T(8,128)S(1)} %pad_maximum_fusion), channel_id=1, source_target_pairs={{0,2},{1,3},{2,4},{3,5},{4,6},{5,7},{6,8},{7,9},{8,10},{9,11},{10,... | collective-permute-start | bytes 786440 | tf_op jit(solution)/shard_map/ppermute | solution.py:19
  100.4 15.1 %collective-permute-start.13 = (f32[128,4,128]{0,2,1:T(8,128)S(1)}, f32[128,4,128]{0,2,1:T(8,128)S(1)}, u32[]{:S(2)}, u32[]{:S(2)}) collective-permute-start(f32[128,4,128]{0,2,1:T(8,128)S(1)} %pad_maximum_fusion), channel_id=1, source_target_pairs={{0,1},{1,2},{2,3},{3,4},{4,5},{5,6},{6,7},{7,8},{8,9},{9,10},{10,1... | collective-permute-start | bytes 786440 | tf_op jit(solution)/shard_map/ppermute | solution.py:19
  100.7 14.8 %collective-permute-start.14 = (f32[128,4,128]{0,2,1:T(8,128)S(1)}, f32[128,4,128]{0,2,1:T(8,128)S(1)}, u32[]{:S(2)}, u32[]{:S(2)}) collective-permute-start(f32[128,4,128]{0,2,1:T(8,128)S(1)} %pad_maximum_fusion), channel_id=1, source_target_pairs={{0,15},{1,0},{2,1},{3,2},{4,3},{5,4},{6,5},{7,6},{8,7},{9,8},{10,9... | collective-permute-start | bytes 786440 | tf_op jit(solution)/shard_map/ppermute | solution.py:19
  105.0 15.7 %collective-permute-start.15 = (f32[128,4,128]{0,2,1:T(8,128)S(1)}, f32[128,4,128]{0,2,1:T(8,128)S(1)}, u32[]{:S(2)}, u32[]{:S(2)}) collective-permute-start(f32[128,4,128]{0,2,1:T(8,128)S(1)} %pad_maximum_fusion), channel_id=1, source_target_pairs={{0,14},{1,15},{2,0},{3,1},{4,2},{5,3},{6,4},{7,5},{8,6},{9,7},{10,... | collective-permute-start | bytes 786440 | tf_op jit(solution)/shard_map/ppermute | solution.py:19
  138.3 65.6 %collective-permute-start.16 = (f32[3,128]{1,0:T(4,128)S(1)}, f32[3,128]{1,0:T(4,128)S(1)}, u32[]{:S(2)}, u32[]{:S(2)}) collective-permute-start(f32[3,128]{1,0:T(4,128)S(1)} %get-tuple-element.128), channel_id=1, source_target_pairs={{0,14},{1,15},{2,0},{3,1},{4,2},{5,3},{6,4},{7,5},{8,6},{9,7},{10,... | collective-permute-start | bytes 4616 | tf_op jit(solution)/shard_map/ppermute | solution.py:19
  141.8 62.1 %collective-permute-start.17 = (f32[3,128]{1,0:T(4,128)S(1)}, f32[3,128]{1,0:T(4,128)S(1)}, u32[]{:S(2)}, u32[]{:S(2)}) collective-permute-start(f32[3,128]{1,0:T(4,128)S(1)} %get-tuple-element.131), channel_id=1, source_target_pairs={{0,15},{1,0},{2,1},{3,2},{4,3},{5,4},{6,5},{7,6},{8,7},{9,8},{10,9... | collective-permute-start | bytes 4616 | tf_op jit(solution)/shard_map/ppermute | solution.py:19
  141.8 62.1 %collective-permute-start.18 = (f32[3,128]{1,0:T(4,128)S(1)}, f32[3,128]{1,0:T(4,128)S(1)}, u32[]{:S(2)}, u32[]{:S(2)}) collective-permute-start(f32[3,128]{1,0:T(4,128)S(1)} %get-tuple-element.130), channel_id=1, source_target_pairs={{0,1},{1,2},{2,3},{3,4},{4,5},{5,6},{6,7},{7,8},{8,9},{9,10},{10,1... | collective-permute-start | bytes 4616 | tf_op jit(solution)/shard_map/ppermute | solution.py:19
  142.3 61.6 %collective-permute-start.19 = (f32[3,128]{1,0:T(4,128)S(1)}, f32[3,128]{1,0:T(4,128)S(1)}, u32[]{:S(2)}, u32[]{:S(2)}) collective-permute-start(f32[3,128]{1,0:T(4,128)S(1)} %get-tuple-element.129), channel_id=1, source_target_pairs={{0,2},{1,3},{2,4},{3,5},{4,6},{5,7},{6,8},{7,9},{8,10},{9,11},{10,... | collective-permute-start | bytes 4616 | tf_op jit(solution)/shard_map/ppermute | solution.py:19
  (156 other events, 564.6 us)
where the time goes:
time: 205 us; the launch traced here: 204 us
  blocking collectives  61.5 us (30%)
  starting transfers between devices  33.3 us (16%)
  matrix products  33.1 us (16%)
  local copies, waits for them, and re-layouts  29.7 us (14%)
  waiting for transfers between devices  26.3 us (13%)
  between operations  11.8 us (6%)
  other arithmetic  8.63 us (4%)
    psum x1, blocking collectives, body(): lax.psum((first_summand, second_summand), 'space')  61.5 us
    ppermute x20, starting transfers between devices, shifted(): return lax.ppermute(value, axis, pairs)  33.3 us
    ppermute x20, waiting for transfers between devices, shifted(): return lax.ppermute(value, axis, pairs)  26.3 us
    unnamed x283, local copies, waits for them, and re-layouts  15.5 us
    dot_general x51, matrix products, contract_trailing(): lax.dot_general(left, right, (((1,), (1,)), ((), ())), preferred_element_...  13.4 us
    dot_general x16, matrix products, tile_messages(): jnp.dot(dir_tile.reshape(3 * atom_count, atom_count), scalars, preferred_...  9.79 us
    slice x48, local copies, waits for them, and re-layouts, tile_messages(): product_all[:, channels:].reshape(atom_count, 3, channels)  8.21 us
    dot_general x16, matrix products, tile_messages(): jnp.dot(dir_tile.reshape(atom_count, 3 * atom_count), vec_stack, preferre...  5.2 us
  transfers between devices with their start and end apart: 20, of which 7 were waited for; matrix products, arithmetic and copies ran while one was open for 5% of the time, Pallas kernels for 0%

commit v1 on v0

v1 whole, which is shorter than its diff:
```python
import functools

import jax
import jax.numpy as jnp
from jax import lax
from jax.experimental import pallas as pl
from jax.experimental.pallas import tpu as pltpu
from jax.sharding import PartitionSpec as P

REACH = 2
WINDOW = 2 * REACH + 1

soft_core = 0.25
centre_start = 1.0
highest = lax.Precision.HIGHEST
MESH = pl.DeviceIdType.MESH
f32 = jnp.float32
bf16 = jnp.bfloat16


def dot(left, right):
    return jnp.dot(left, right, preferred_element_type=f32)


def dot_trailing(left, right):
    return lax.dot_general(left, right, (((1,), (1,)), ((), ())), preferred_element_type=f32)


def kernel(
    count,
    rounds,
    table_ref,
    live_ref,
    feat_ref,
    pos_ref,
    species_ref,
    mask_ref,
    radial_ref,
    scale_ref,
    mix_ref,
    down_ref,
    up_ref,
    readout_ref,
    weight_ref,
    energy_ref,
    coord_ref,
    down_grad_ref,
    up_grad_ref,
    feat_win,
    cot_win,
    pos_win,
    partial,
    sib_out,
    sib_in,
    far_out,
    far_in,
    near_out,
    near_in,
    lefts,
    masked_buf,
    dist_buf,
    unit_buf,
    acc,
    grad_dist,
    grad_unit,
    scale_buf,
    table_pad,
    grad_out,
    grad_in,
    ring_out,
    ring_in,
    feat_send,
    feat_recv,
    cot_send,
    cot_recv,
    pos_send,
    pos_recv,
    msg_send,
    msg_recv,
    grad_send,
    grad_recv,
    ring_send,
    ring_recv,
):
    comps, atoms, channels = feat_ref.shape
    slots = mask_ref.shape[0]
    basis = radial_ref.shape[1]
    me = lax.axis_index("space")
    core = lax.rem(me, 2)
    col = lax.rem(me // 2, 2)
    sib = me + 1 - 2 * core
    near = me + 2 - 4 * col
    onward = lax.rem(me + 4 - 8 * col + count, count)
    behind = lax.rem(me - 4 + 8 * col + count, count)
    near_slot = 4 - 4 * col
    far_slot = 4 * col
    sib_slot = 3 - 2 * core
    oth_slot = 1 + 2 * core
    through_slot = 4 - 4 * core

    def partner(level):
        step = 1 << level
        return me + step - 2 * step * lax.rem(me // step, 2)

    def offset(steps):
        return lax.rem(me + steps + count, count)

    def remote(src, dst, send, recv, device):
        return pltpu.make_async_remote_copy(
            src_ref=src,
            dst_ref=dst,
            send_sem=send,
            recv_sem=recv,
            device_id={"space": device},
            device_id_type=MESH,
        )

    barrier = pltpu.get_barrier_semaphore()
    greeted = [offset(steps) for steps in (-1, 1, -2, 2, -4, 4)]
    greeted += [partner(level) for level in range(3, rounds)]
    for device in greeted:
        pl.semaphore_signal(barrier, inc=1, device_id={"space": device}, device_id_type=MESH)

    feat_win[2] = feat_ref[...]
    pos_win[2] = jnp.zeros(pos_win.shape[1:], f32)
    pos_win[2, 0:3] = pos_ref[...]
    table_pad[...] = jnp.zeros(table_pad.shape, f32)
    table_pad[0 : scale_ref.shape[0]] = scale_ref[...]

    pl.semaphore_wait(barrier, len(greeted))

    def cast_start(win, send, recv):
        copies = []
        for j in range(comps):
            copies.append(
                remote(win.at[2, j], win.at[far_slot, j], send.at[0, j], recv.at[far_slot, j], near)
            )
            copies[-1].start()
        for j in range(comps):
            copies.append(
                remote(win.at[2, j], win.at[oth_slot, j], send.at[1, j], recv.at[oth_slot, j], sib)
            )
            copies[-1].start()
        return copies

    def arrived(win, send, recv, slot, j):
        remote(win.at[2, j], win.at[slot, j], send.at[0, j], recv.at[slot, j], near).wait_recv()

    def cast_relay(win, send, recv):
        copies = []
        for j in range(comps):
            arrived(win, send, recv, near_slot, j)
            copies.append(
                remote(
                    win.at[near_slot, j],
                    win.at[far_slot, j],
                    send.at[2, j],
                    recv.at[far_slot, j],
                    onward,
                )
            )
            copies[-1].start()
        return copies

    def cast_finish(win, send, recv):
        copies = []
        for j in range(comps):
            arrived(win, send, recv, far_slot, j)
            copies.append(
                remote(
                    win.at[through_slot, j],
                    win.at[sib_slot, j],
                    send.at[3, j],
                    recv.at[sib_slot, j],
                    sib,
                )
            )
            copies[-1].start()
        for j in range(comps):
            arrived(win, send, recv, sib_slot, j)
            arrived(win, send, recv, oth_slot, j)
        return copies

    pending = []
    pos_copies = []
    for w in (0, 1, 3, 4):
        copy = remote(
            pos_win.at[2],
            pos_win.at[4 - w],
            pos_send.at[w],
            pos_recv.at[4 - w],
            offset(w - 2),
        )
        copy.start()
        pos_copies.append(copy)
    pending += cast_start(feat_win, feat_send, feat_recv)

    species_cols = lax.broadcasted_iota(jnp.int32, (atoms, atoms), 0) == species_ref[...]
    one_hot = jnp.transpose(species_cols.astype(f32))
    scale_buf[...] = jnp.dot(
        one_hot, table_pad[...], precision=highest, preferred_element_type=f32
    )

    def window_of(block):
        return jnp.clip(lax.rem(block - me + REACH + 2 * count, count), 0, 2 * REACH)

    recv_idx = [window_of(table_ref[0, s]) for s in range(slots)]
    send_idx = [window_of(table_ref[1, s]) for s in range(slots)]
    live = [jnp.where(s < live_ref[0], 1.0, 0.0).astype(f32) for s in range(slots)]

    for copy in pos_copies:
        copy.wait_send()
    for w in (0, 1, 3, 4):
        remote(
            pos_win.at[2], pos_win.at[w], pos_send.at[w], pos_recv.at[w], offset(w - 2)
        ).wait_recv()

    pending += cast_relay(feat_win, feat_send, feat_recv)

    for s in range(slots):
        columns = jnp.transpose(pos_win[recv_idx[s]])
        rows = pos_win[send_idx[s]]
        offsets = [rows[x : x + 1, :] - columns[:, x : x + 1] for x in range(3)]
        dist = jnp.sqrt(
            offsets[0] * offsets[0] + offsets[1] * offsets[1] + offsets[2] * offsets[2] + soft_core
        )
        inverse = 1.0 / dist
        dist_buf[s] = dist
        for x in range(3):
            unit_buf[s, x] = offsets[x] * inverse

        def build(k, carry, s=s):
            scaled = dist_buf[s] - (centre_start + k.astype(f32))
            masked = jnp.exp(-scaled * scaled) * mask_ref[s].astype(f32)
            masked_buf[s, k] = masked
            lefts[s, k, 0] = masked.astype(bf16)
            for x in range(3):
                lefts[s, k, 1 + x] = (masked * unit_buf[s, x]).astype(bf16)
            return carry

        lax.fori_loop(0, basis, build, 0)

    pending += cast_finish(feat_win, feat_send, feat_recv)

    for s in range(slots):
        sent = feat_win[send_idx[s]]
        wide = jnp.concatenate([sent[j] for j in range(4)], axis=1)
        tall = sent[1:].reshape(3 * atoms, channels)

        def messages(k, carry, s=s, wide=wide, tall=tall, sent=sent):
            left = lefts[s, k]
            weight = [radial_ref[path, pl.ds(k, 1), :] for path in range(4)]
            plain = dot(left[0], wide)
            along = dot(left[1:].reshape(3 * atoms, atoms), sent[0])
            inner = dot(jnp.concatenate([left[1], left[2], left[3]], axis=1), tall)
            acc[s, 0] += weight[0] * plain[:, :channels] + weight[1] * inner
            for x in range(3):
                acc[s, 1 + x] += (
                    weight[2] * along[x * atoms : (x + 1) * atoms]
                    + weight[3] * plain[:, (1 + x) * channels : (2 + x) * channels]
                )
            return carry

        acc[s] = jnp.zeros(acc.shape[1:], f32)
        lax.fori_loop(0, basis, messages, 0)

    share = [
        [jnp.where(recv_idx[s] == w, live[s], 0.0) for s in range(slots)] for w in range(WINDOW)
    ]
    for j in range(comps):
        for w in range(WINDOW):
            total = share[w][0] * acc[0, j]
            for s in range(1, slots):
                total = total + share[w][s] * acc[s, j]
            partial[w, j] = total
        sib_out[j, 0] = partial[oth_slot, j]
        sib_out[j, 1] = partial[sib_slot, j]
        copy = remote(sib_out.at[j], sib_in.at[j], msg_send.at[0, j], msg_recv.at[0, j], sib)
        copy.start()
        pending.append(copy)

    for j in range(comps):
        remote(sib_out.at[j], sib_in.at[j], msg_send.at[0, j], msg_recv.at[0, j], sib).wait_recv()
        partial[through_slot, j] += sib_in[j, 0]
        far_out[j] = partial[far_slot, j]
        copy = remote(far_out.at[j], far_in.at[j], msg_send.at[1, j], msg_recv.at[1, j], behind)
        copy.start()
        pending.append(copy)
    for j in range(comps):
        remote(far_out.at[j], far_in.at[j], msg_send.at[1, j], msg_recv.at[1, j], behind).wait_recv()
        near_out[j] = partial[near_slot, j] + far_in[j]
        copy = remote(near_out.at[j], near_in.at[j], msg_send.at[2, j], msg_recv.at[2, j], near)
        copy.start()
        pending.append(copy)
    gathered = []
    for j in range(comps):
        remote(near_out.at[j], near_in.at[j], msg_send.at[2, j], msg_recv.at[2, j], near).wait_recv()
        gathered.append(partial[2, j] + sib_in[j, 1] + near_in[j])

    scale = scale_buf[...]
    squares = gathered[1] * gathered[1] + gathered[2] * gathered[2] + gathered[3] * gathered[3]
    invariant = (scale * (gathered[0] + squares)).astype(bf16)
    low_rank = dot(invariant, down_ref[...]).astype(bf16)
    hidden = dot(invariant, mix_ref[...]) + dot(low_rank, up_ref[...])
    sigma = jax.nn.sigmoid(hidden)
    weight_cols = jnp.transpose(jnp.broadcast_to(weight_ref[...], (atoms, atoms)))
    if channels != atoms:
        weight_cols = jnp.broadcast_to(weight_cols[:, :1], (atoms, channels))
    slope = sigma * (1.0 + hidden * (1.0 - sigma))
    grad_pre = (weight_cols * readout_ref[...] * slope).astype(bf16)
    grad_low = dot_trailing(grad_pre, up_ref[...]).astype(bf16)
    grad_inv = dot_trailing(grad_pre, mix_ref[...]) + dot_trailing(grad_low, down_ref[...])
    seed = scale * grad_inv
    cot_win[2, 0] = seed.astype(bf16)
    for x in range(3):
        cot_win[2, 1 + x] = (2.0 * seed * gathered[1 + x]).astype(bf16)
    pending += cast_start(cot_win, cot_send, cot_recv)

    rank = up_ref.shape[0]
    ring_out[0, 0:rank] = dot(jnp.transpose(grad_low.astype(f32)).astype(bf16), invariant)
    ring_out[0, rank:] = dot(jnp.transpose(low_rank.astype(f32)).astype(bf16), grad_pre)
    energy_ref[...] = jnp.sum(
        jnp.transpose(hidden * sigma * readout_ref[...]), axis=0, keepdims=True
    )

    def ring_copy(level):
        return remote(
            ring_out.at[level],
            ring_in.at[level],
            ring_send.at[level],
            ring_recv.at[level],
            partner(level),
        )

    def ring_start(level):
        copy = ring_copy(level)
        copy.start()
        pending.append(copy)

    def ring_finish(level):
        ring_copy(level).wait_recv()
        ring_out[level + 1] = ring_out[level] + ring_in[level]

    ring_start(0)
    pending += cast_relay(cot_win, cot_send, cot_recv)
    ring_finish(0)
    ring_start(1)
    pending += cast_finish(cot_win, cot_send, cot_recv)

    lanes = lax.broadcasted_iota(jnp.int32, (atoms, atoms), 1)
    row_ids = lax.broadcasted_iota(jnp.int32, (8, atoms), 0)
    recv_grads, send_grads = [], []
    for s in range(slots):
        sent = feat_win[send_idx[s]]
        wide = jnp.concatenate([sent[j] for j in range(4)], axis=1)
        pairs = [jnp.concatenate([sent[0], sent[1 + x]], axis=1) for x in range(3)]

        def gradients(k, carry, s=s, wide=wide, pairs=pairs):
            weight = [radial_ref[path, pl.ds(k, 1), :] for path in range(4)]
            cot = [cot_win[recv_idx[s], j].astype(f32) for j in range(4)]
            wall = jnp.concatenate(
                [(weight[0] * cot[0]).astype(bf16)]
                + [(weight[3] * cot[1 + x]).astype(bf16) for x in range(3)],
                axis=1,
            )
            inner = (weight[1] * cot[0]).astype(bf16)
            total = dot_trailing(wall, wide)
            masked = masked_buf[s, k]
            for x in range(3):
                along = (weight[2] * cot[1 + x]).astype(bf16)
                grad_dir = dot_trailing(jnp.concatenate([along, inner], axis=1), pairs[x])
                total = total + grad_dir * unit_buf[s, x]
                grad_unit[x] += masked * grad_dir
            scaled = dist_buf[s] - (centre_start + k.astype(f32))
            grad_dist[...] += total * masked * (-2.0 * scaled)
            return carry

        grad_dist[...] = jnp.zeros(grad_dist.shape, f32)
        grad_unit[...] = jnp.zeros(grad_unit.shape, f32)
        lax.fori_loop(0, basis, gradients, 0)
        units = [unit_buf[s, x] for x in range(3)]
        dirs = [grad_unit[x] for x in range(3)]
        radial_part = dirs[0] * units[0] + dirs[1] * units[1] + dirs[2] * units[2]
        inverse = 1.0 / dist_buf[s]
        columns = jnp.zeros((atoms, atoms), f32)
        send_rows = jnp.zeros((8, atoms), f32)
        for x in range(3):
            grad = grad_dist[...] * units[x] + (dirs[x] - units[x] * radial_part) * inverse
            columns = jnp.where(lanes == x, jnp.sum(grad, axis=1, keepdims=True), columns)
            send_rows = jnp.where(row_ids == x, jnp.sum(grad, axis=0, keepdims=True), send_rows)
        recv_grads.append(-jnp.transpose(columns)[0:8])
        send_grads.append(send_rows)
        if s + 1 < min(rounds, slots):
            ring_finish(s + 1)
            ring_start(s + 2)

    for w in range(WINDOW):
        total = jnp.zeros((8, atoms), f32)
        for s in range(slots):
            total = total + share[w][s] * recv_grads[s]
            total = total + jnp.where(send_idx[s] == w, live[s], 0.0) * send_grads[s]
        grad_out[w] = total
    for w in (0, 1, 3, 4):
        copy = remote(
            grad_out.at[w],
            grad_in.at[4 - w],
            grad_send.at[w],
            grad_recv.at[4 - w],
            offset(w - 2),
        )
        copy.start()
        pending.append(copy)
    for level in range(slots, rounds):
        ring_finish(level)
        if level + 1 < rounds:
            ring_start(level + 1)
    coord = grad_out[2]
    for w in (0, 1, 3, 4):
        remote(
            grad_out.at[w], grad_in.at[w], grad_send.at[w], grad_recv.at[w], offset(w - 2)
        ).wait_recv()
        coord = coord + grad_in[w]
    coord_ref[...] = coord[0:3]
    down_grad_ref[...] = jnp.transpose(ring_out[rounds, 0:rank])
    up_grad_ref[...] = ring_out[rounds, rank:]
    for copy in pending:
        copy.wait_send()


def body(
    features,
    positions,
    species,
    block_pair_table,
    device_pair_count,
    edge_tile_masks,
    radial,
    element_scale_table,
    linear_mixing_weight,
    down_adapter_weight,
    up_adapter_weight,
    readout_weight,
    atom_energy_weight,
):
    count = lax.axis_size("space")
    rounds = count.bit_length() - 1
    assert count == 1 << rounds and rounds >= 3
    atoms, comps, channels = features.shape
    slots = edge_tile_masks.shape[0]
    basis = radial.shape[1]
    rank = up_adapter_weight.shape[0]
    vmem = pl.BlockSpec(memory_space=pltpu.VMEM)
    smem = pl.BlockSpec(memory_space=pltpu.SMEM)
    dma = pltpu.SemaphoreType.DMA
    block = (comps, atoms, channels)
    energies, coordinate_gradient, down_gradient, up_gradient = pl.pallas_call(
        functools.partial(kernel, count, rounds),
        out_shape=(
            jax.ShapeDtypeStruct((1, atoms), f32),
            jax.ShapeDtypeStruct((3, atoms), f32),
            jax.ShapeDtypeStruct((channels, rank), f32),
            jax.ShapeDtypeStruct((rank, channels), f32),
        ),
        in_specs=[smem, smem] + [vmem] * 11,
        out_specs=(vmem,) * 4,
        scratch_shapes=[
            pltpu.VMEM((WINDOW,) + block, bf16),
            pltpu.VMEM((WINDOW,) + block, bf16),
            pltpu.VMEM((WINDOW, 8, atoms), f32),
            pltpu.VMEM((WINDOW,) + block, f32),
            pltpu.VMEM((comps, 2, atoms, channels), f32),
            pltpu.VMEM((comps, 2, atoms, channels), f32),
            pltpu.VMEM(block, f32),
            pltpu.VMEM(block, f32),
            pltpu.VMEM(block, f32),
            pltpu.VMEM(block, f32),
            pltpu.VMEM((slots, basis, 4, atoms, atoms), bf16),
            pltpu.VMEM((slots, basis, atoms, atoms), f32),
            pltpu.VMEM((slots, atoms, atoms), f32),
            pltpu.VMEM((slots, 3, atoms, atoms), f32),
            pltpu.VMEM((slots,) + block, f32),
            pltpu.VMEM((atoms, atoms), f32),
            pltpu.VMEM((3, atoms, atoms), f32),
            pltpu.VMEM((atoms, channels), f32),
            pltpu.VMEM((128, channels), f32),
            pltpu.VMEM((WINDOW, 8, atoms), f32),
            pltpu.VMEM((WINDOW, 8, atoms), f32),
            pltpu.VMEM((rounds + 1, 2 * rank, channels), f32),
            pltpu.VMEM((rounds, 2 * rank, channels), f32),
            dma((4, comps)),
            dma((WINDOW, comps)),
            dma((4, comps)),
            dma((WINDOW, comps)),
            dma((WINDOW,)),
            dma((WINDOW,)),
            dma((3, comps)),
            dma((3, comps)),
            dma((WINDOW,)),
            dma((WINDOW,)),
            dma((rounds,)),
            dma((rounds,)),
        ],
        compiler_params=pltpu.CompilerParams(
            collective_id=0, has_side_effects=True, vmem_limit_bytes=40 * 1024 * 1024
        ),
    )(
        block_pair_table,
        device_pair_count,
        jnp.transpose(features, (1, 0, 2)),
        positions,
        species.reshape(1, atoms),
        edge_tile_masks,
        radial,
        element_scale_table,
        linear_mixing_weight,
        down_adapter_weight,
        up_adapter_weight,
        readout_weight.reshape(1, channels),
        atom_energy_weight.reshape(1, atoms),
    )
    return (energies.reshape(atoms), coordinate_gradient, down_gradient, up_gradient)


def solution(mesh):
    placed = (
        P(("groups", "space"), None, None),
        P(None, ("groups", "space")),
        P(("groups", "space")),
        P(None, ("groups", "space")),
        P(("groups", "space")),
        P(("groups", "space"), None, None),
        P(),
        P(),
        P(),
        P(),
        P(),
        P(),
        P(("groups", "space")),
    )
    return jax.shard_map(
        body,
        mesh=mesh,
        in_specs=placed,
        out_specs=(
            P(("groups", "space")),
            P(None, ("groups", "space")),
            P("groups", None),
            P("groups", None),
        ),
        check_vma=False,
    )
```

time: 205 us -> 57.9 us (0.28)
  blocking collectives: 61.5 us -> 0 us
  Pallas kernels: 0 us -> 52.1 us
  starting transfers between devices: 33.3 us -> 0 us
  matrix products: 33.1 us -> 0 us
  waiting for transfers between devices: 26.3 us -> 0 us
  local copies, waits for them, and re-layouts: 29.7 us -> 4.15 us
  between operations: 11.8 us -> 1.45 us
  other arithmetic: 8.63 us -> 0 us
    psum x1 -> x0, blocking collectives: 61.5 us -> none  [body(): lax.psum((first_summand, second_summand), 'space')]
    pallas_call x0 -> x1, Pallas kernels: none -> 52.1 us  [body(): pl.pallas_call(functools.partial(kernel, count, rounds), out_shape=(jax.S...]
    ppermute x20 -> x0, starting transfers between devices: 33.3 us -> none  [shifted(): return lax.ppermute(value, axis, pairs)]
    dot_general x106 -> x0, matrix products: 33.1 us -> none  [the longest x51 13.4 us: contract_trailing(): lax.dot_general(left, right, (((1,), (1,)), ((), ())), preferred_element_...]
    ppermute x20 -> x0, waiting for transfers between devices: 26.3 us -> none  [shifted(): return lax.ppermute(value, axis, pairs)]
    unnamed x283 -> x28, local copies, waits for them, and re-layouts: 15.5 us -> 4.15 us
    slice x83 -> x0, local copies, waits for them, and re-layouts: 10.3 us -> none  [the longest x48 8.21 us: tile_messages(): product_all[:, channels:].reshape(atom_count, 3, channels)]
    dynamic_update_slice x6 -> x0, other arithmetic: 3.66 us -> none  [window_add(): lax.dynamic_update_index_in_dim(window_buf, current + value, index, 0)]
  transfers between devices with their start and end apart: 20 -> 0, of which waited for: 7 -> 0; matrix products, arithmetic and copies ran while one was open for 5% -> 0% of each run, Pallas kernels for 0% -> 0%
where the time goes in v1:
time: 57.9 us; the launch traced here: 57.7 us
  Pallas kernels  52.1 us (90%)
  local copies, waits for them, and re-layouts  4.15 us (7%)
  between operations  1.45 us (3%)
    pallas_call x1, Pallas kernels, body(): pl.pallas_call(functools.partial(kernel, count, rounds), out_shape=(jax.S...  52.1 us
    unnamed x28, local copies, waits for them, and re-layouts  4.15 us

profile of v1, /device:TPU:0, one launch (start us, length us, event | category | flops | bytes accessed | tf_op | source)
XLA Modules:
  0.0 57.7 jit_solution(3768079045479928764)
XLA Ops:
  0.6 0.0 copy-start.10
  1.3 0.0 copy-done.10
  1.3 0.1 copy.18.down_ref
  1.4 0.0 copy-start.1
  1.5 0.0 copy-start.2
  1.5 0.0 copy-start.3
  1.5 0.0 copy-start.4
  1.5 0.0 copy-start.5
  1.5 0.0 copy-start.8
  1.5 0.0 copy-start.9
  1.5 1.0 %copy.21 = bf16[128,4,128]{2,0,1:T(8,128)(2,1)S(1)} copy(bf16[128,4,128]{2,1,0:T(4,128)(2,1)} %param.13) | data formatting | bytes 262144 | tf_op args[0]
  2.6 0.0 copy-start.6
  2.6 0.0 copy-start.7
  2.6 0.0 copy-done
  2.6 0.0 copy-done.1
  2.6 0.0 copy-done.2
  2.6 0.0 copy-done.3
  2.6 0.0 copy-done.4
  2.7 0.6 %copy-done.6 = s32[2,2]{1,0:T(2,128)S(1)} copy-done((s32[2,2]{1,0:T(2,128)S(1)}, s32[2,2]{1,0:T(2,128)}, u32[]{:S(2)}) %copy-start.6) | copy-done | bytes 40
  3.2 52.1 %shard_map.156 = (f32[1,128]{1,0:T(1,128)S(1)}, f32[3,128]{1,0:T(4,128)S(1)}, f32[128,16]{1,0:T(8,128)S(1)}, f32[16,128]{1,0:T(8,128)S(1)}) custom-call(s32[2,2]{1,0:T(2,128)S(1)} %copy-done.6, s32[1]{0:T(128)S(6)} %copy.25.live_ref, bf16[4,128,128]{2,1,0:T(8,128)(2,1)S(1)} %bitcast.7, f32[3,128]{1,0:T(4,128)S(1)} %copy-done.5, s32[1,128]{1,0:T(1,128)S(1)} %bitcast.8, ...), custom_call_target="tpu_custom_call" | custom-call | tf_op jit(solution)/shard_map/pallas_call | solution.py:456
  55.4 0.7 %copy.19 = f32[128,16]{0,1:T(8,128)} copy(f32[128,16]{1,0:T(8,128)S(1)} %get-tuple-element.14) | data formatting | bytes 16384
  56.0 0.5 copy.26
  56.5 0.6 %copy.27 = f32[3,128]{1,0:T(4,128)} copy(f32[3,128]{1,0:T(4,128)S(1)} %get-tuple-element.21) | data formatting | bytes 3072
  57.1 0.6 %copy.28 = f32[16,128]{1,0:T(8,128)} copy(f32[16,128]{1,0:T(8,128)S(1)} %get-tuple-element.23) | data formatting | bytes 16384
  (5 shorter events, 0.0 us)
Async XLA Ops:
  0.6 0.7 %copy-start.10 = (bf16[128,16]{0,1:T(8,128)(2,1)S(1)}, bf16[128,16]{0,1:T(8,128)(2,1)}, u32[]{:S(2)}) copy-start(bf16[128,16]{0,1:T(8,128)(2,1)} %param.22) | copy-start | bytes 12292
  1.4 1.1 %copy-start = (s32[2,128,128]{2,1,0:T(8,128)S(1)}, s32[2,128,128]{2,1,0:T(8,128)}, u32[]{:S(2)}) copy-start(s32[2,128,128]{2,1,0:T(8,128)} %mask_ref.1) | copy-start | bytes 393220
  1.4 1.1 %copy-start.1 = (f32[89,128]{1,0:T(8,128)S(1)}, f32[89,128]{1,0:T(8,128)}, u32[]{:S(2)}) copy-start(f32[89,128]{1,0:T(8,128)} %scale_ref.1) | copy-start | bytes 136708
  1.5 1.1 %copy-start.2 = (bf16[128,128]{1,0:T(8,128)(2,1)S(1)}, bf16[128,128]{1,0:T(8,128)(2,1)}, u32[]{:S(2)}) copy-start(bf16[128,128]{1,0:T(8,128)(2,1)} %mix_ref.1) | copy-start | bytes 98308
  1.5 1.1 %copy-start.3 = (f32[4,8,128]{2,1,0:T(8,128)S(1)}, f32[4,8,128]{2,1,0:T(8,128)}, u32[]{:S(2)}) copy-start(f32[4,8,128]{2,1,0:T(8,128)} %radial_ref.1) | copy-start | bytes 49156
  1.5 1.1 %copy-start.4 = (bf16[16,128]{1,0:T(8,128)(2,1)S(1)}, bf16[16,128]{1,0:T(8,128)(2,1)}, u32[]{:S(2)}) copy-start(bf16[16,128]{1,0:T(8,128)(2,1)} %up_ref.1) | copy-start | bytes 12292
  1.5 1.1 %copy-start.5 = (f32[3,128]{1,0:T(4,128)S(1)}, f32[3,128]{1,0:T(4,128)}, u32[]{:S(2)}) copy-start(f32[3,128]{1,0:T(4,128)} %pos_ref.1) | copy-start | bytes 4612
  1.5 1.1 %copy-start.8 = (f32[128]{0:T(128)S(1)}, f32[128]{0:T(128)}, u32[]{:S(2)}) copy-start(f32[128]{0:T(128)} %param.24) | copy-start | bytes 1540
  1.5 1.1 %copy-start.9 = (f32[128]{0:T(128)S(1)}, f32[128]{0:T(128)}, u32[]{:S(2)}) copy-start(f32[128]{0:T(128)} %param.25) | copy-start | bytes 1540
  2.6 0.7 %copy-start.6 = (s32[2,2]{1,0:T(2,128)S(1)}, s32[2,2]{1,0:T(2,128)}, u32[]{:S(2)}) copy-start(s32[2,2]{1,0:T(2,128)} %table_ref.1) | copy-start | bytes 52
  2.6 0.7 %copy-start.7 = (s32[128]{0:T(128)S(1)}, s32[128]{0:T(128)}, u32[]{:S(2)}) copy-start(s32[128]{0:T(128)} %param.15) | copy-start | bytes 1540

commit v2 on v1

--- a/solution.py
+++ b/solution.py
@@ -44,25 +44,18 @@
     weight_ref,
     energy_ref,
     coord_ref,
-    down_grad_ref,
-    up_grad_ref,
+    adapter_ref,
     feat_win,
-    cot_win,
+    agg_win,
     pos_win,
     partial,
-    sib_out,
     sib_in,
-    far_out,
     far_in,
-    near_out,
     near_in,
     lefts,
     masked_buf,
     dist_buf,
     unit_buf,
-    acc,
-    grad_dist,
-    grad_unit,
     scale_buf,
     table_pad,
     grad_out,
@@ -129,26 +122,22 @@
 
     pl.semaphore_wait(barrier, len(greeted))
 
-    def cast_start(win, send, recv):
+    def cast_start(win, send, recv, parts):
         copies = []
-        for j in range(comps):
-            copies.append(
-                remote(win.at[2, j], win.at[far_slot, j], send.at[0, j], recv.at[far_slot, j], near)
-            )
-            copies[-1].start()
-        for j in range(comps):
-            copies.append(
-                remote(win.at[2, j], win.at[oth_slot, j], send.at[1, j], recv.at[oth_slot, j], sib)
-            )
-            copies[-1].start()
+        for target, slot, kind in ((near, far_slot, 0), (sib, oth_slot, 1)):
+            for j in parts:
+                copies.append(
+                    remote(win.at[2, j], win.at[slot, j], send.at[kind, j], recv.at[slot, j], target)
+                )
+                copies[-1].start()
         return copies
 
     def arrived(win, send, recv, slot, j):
         remote(win.at[2, j], win.at[slot, j], send.at[0, j], recv.at[slot, j], near).wait_recv()
 
-    def cast_relay(win, send, recv):
+    def cast_relay(win, send, recv, parts):
         copies = []
-        for j in range(comps):
+        for j in parts:
             arrived(win, send, recv, near_slot, j)
             copies.append(
                 remote(
@@ -162,9 +151,9 @@
             copies[-1].start()
         return copies
 
-    def cast_finish(win, send, recv):
+    def cast_forward(win, send, recv, parts):
         copies = []
-        for j in range(comps):
+        for j in parts:
             arrived(win, send, recv, far_slot, j)
             copies.append(
                 remote(
@@ -176,11 +165,14 @@
                 )
             )
             copies[-1].start()
-        for j in range(comps):
+        return copies
+
+    def cast_finish(win, send, recv, parts):
+        for j in parts:
             arrived(win, send, recv, sib_slot, j)
             arrived(win, send, recv, oth_slot, j)
-        return copies
-
+
+    order = (1, 2, 3, 0)
     pending = []
     pos_copies = []
     for w in (0, 1, 3, 4):
@@ -193,7 +185,7 @@
         )
         copy.start()
         pos_copies.append(copy)
-    pending += cast_start(feat_win, feat_send, feat_recv)
+    pending += cast_start(feat_win, feat_send, feat_recv, range(comps))
 
     species_cols = lax.broadcasted_iota(jnp.int32, (atoms, atoms), 0) == species_ref[...]
     one_hot = jnp.transpose(species_cols.astype(f32))
@@ -215,7 +207,7 @@
             pos_win.at[2], pos_win.at[w], pos_send.at[w], pos_recv.at[w], offset(w - 2)
         ).wait_recv()
 
-    pending += cast_relay(feat_win, feat_send, feat_recv)
+    pending += cast_relay(feat_win, feat_send, feat_recv, range(comps))
 
     for s in range(slots):
         columns = jnp.transpose(pos_win[recv_idx[s]])
@@ -233,69 +225,97 @@
             scaled = dist_buf[s] - (centre_start + k.astype(f32))
             masked = jnp.exp(-scaled * scaled) * mask_ref[s].astype(f32)
             masked_buf[s, k] = masked
-            lefts[s, k, 0] = masked.astype(bf16)
+            lefts[s, 0, k] = masked.astype(bf16)
             for x in range(3):
-                lefts[s, k, 1 + x] = (masked * unit_buf[s, x]).astype(bf16)
+                lefts[s, 1 + x, k] = (masked * unit_buf[s, x]).astype(bf16)
             return carry
 
         lax.fori_loop(0, basis, build, 0)
 
-    pending += cast_finish(feat_win, feat_send, feat_recv)
-
-    for s in range(slots):
-        sent = feat_win[send_idx[s]]
-        wide = jnp.concatenate([sent[j] for j in range(4)], axis=1)
-        tall = sent[1:].reshape(3 * atoms, channels)
-
-        def messages(k, carry, s=s, wide=wide, tall=tall, sent=sent):
-            left = lefts[s, k]
-            weight = [radial_ref[path, pl.ds(k, 1), :] for path in range(4)]
-            plain = dot(left[0], wide)
-            along = dot(left[1:].reshape(3 * atoms, atoms), sent[0])
-            inner = dot(jnp.concatenate([left[1], left[2], left[3]], axis=1), tall)
-            acc[s, 0] += weight[0] * plain[:, :channels] + weight[1] * inner
-            for x in range(3):
-                acc[s, 1 + x] += (
-                    weight[2] * along[x * atoms : (x + 1) * atoms]
-                    + weight[3] * plain[:, (1 + x) * channels : (2 + x) * channels]
-                )
-            return carry
-
-        acc[s] = jnp.zeros(acc.shape[1:], f32)
-        lax.fori_loop(0, basis, messages, 0)
+    pending += cast_forward(feat_win, feat_send, feat_recv, range(comps))
+    cast_finish(feat_win, feat_send, feat_recv, range(comps))
 
     share = [
         [jnp.where(recv_idx[s] == w, live[s], 0.0) for s in range(slots)] for w in range(WINDOW)
     ]
-    for j in range(comps):
+
+    def weighted(product, path):
+        total = radial_ref[path, 0:1, :] * product[0:atoms]
+        for k in range(1, basis):
+            total = total + radial_ref[path, k : k + 1, :] * product[k * atoms : (k + 1) * atoms]
+        return total
+
+    def component(j):
+        terms = []
+        for s in range(slots):
+            plain = lefts[s, 0].reshape(basis * atoms, atoms)
+            straight = dot(plain, feat_win[send_idx[s], j])
+            if j == 0:
+                turned = [lefts[s, 1 + x].reshape(basis * atoms, atoms) for x in range(3)]
+                tall = feat_win[send_idx[s]][1:].reshape(3 * atoms, channels)
+                crossed = dot(jnp.concatenate(turned, axis=1), tall)
+                terms.append(weighted(straight, 0) + weighted(crossed, 1))
+            else:
+                turned = lefts[s, j].reshape(basis * atoms, atoms)
+                crossed = dot(turned, feat_win[send_idx[s], 0])
+                terms.append(weighted(crossed, 2) + weighted(straight, 3))
         for w in range(WINDOW):
-            total = share[w][0] * acc[0, j]
+            total = share[w][0] * terms[0]
             for s in range(1, slots):
-                total = total + share[w][s] * acc[s, j]
+                total = total + share[w][s] * terms[s]
             partial[w, j] = total
-        sib_out[j, 0] = partial[oth_slot, j]
-        sib_out[j, 1] = partial[sib_slot, j]
-        copy = remote(sib_out.at[j], sib_in.at[j], msg_send.at[0, j], msg_recv.at[0, j], sib)
+
+    def message_copy(hop, j):
+        src, dst, device = (
+            (partial.at[oth_slot, j], sib_in.at[0, j], sib),
+            (partial.at[sib_slot, j], sib_in.at[1, j], sib),
+            (partial.at[far_slot, j], far_in.at[j], behind),
+            (partial.at[near_slot, j], near_in.at[j], near),
+        )[hop]
+        return remote(src, dst, msg_send.at[hop, j], msg_recv.at[hop, j], device)
+
+    def message_start(hop, j):
+        copy = message_copy(hop, j)
         copy.start()
         pending.append(copy)
 
-    for j in range(comps):
-        remote(sib_out.at[j], sib_in.at[j], msg_send.at[0, j], msg_recv.at[0, j], sib).wait_recv()
-        partial[through_slot, j] += sib_in[j, 0]
-        far_out[j] = partial[far_slot, j]
-        copy = remote(far_out.at[j], far_in.at[j], msg_send.at[1, j], msg_recv.at[1, j], behind)
-        copy.start()
-        pending.append(copy)
-    for j in range(comps):
-        remote(far_out.at[j], far_in.at[j], msg_send.at[1, j], msg_recv.at[1, j], behind).wait_recv()
-        near_out[j] = partial[near_slot, j] + far_in[j]
-        copy = remote(near_out.at[j], near_in.at[j], msg_send.at[2, j], msg_recv.at[2, j], near)
-        copy.start()
-        pending.append(copy)
-    gathered = []
-    for j in range(comps):
-        remote(near_out.at[j], near_in.at[j], msg_send.at[2, j], msg_recv.at[2, j], near).wait_recv()
-        gathered.append(partial[2, j] + sib_in[j, 1] + near_in[j])
+    def to_sib(j):
+        component(j)
+        message_start(0, j)
+        message_start(1, j)
+
+    def to_far(j):
+        message_copy(0, j).wait_recv()
+        partial[through_slot, j] += sib_in[0, j]
+        message_start(2, j)
+
+    def to_near(j):
+        message_copy(2, j).wait_recv()
+        partial[near_slot, j] += far_in[j]
+        message_start(3, j)
+
+    def gather(j):
+        message_copy(1, j).wait_recv()
+        message_copy(3, j).wait_recv()
+        return partial[2, j] + sib_in[1, j] + near_in[j]
+
+    to_sib(1)
+    to_sib(2)
+    to_far(1)
+    to_sib(3)
+    to_far(2)
+    to_sib(0)
+    to_near(1)
+    to_far(3)
+    to_far(0)
+    to_near(2)
+    to_near(3)
+    for j in (1, 2, 3):
+        agg_win[2, j] = gather(j)
+        pending += cast_start(agg_win, cot_send, cot_recv, (j,))
+        if j == 1:
+            to_near(0)
+    gathered = [gather(0)] + [agg_win[2, j] for j in (1, 2, 3)]
 
     scale = scale_buf[...]
     squares = gathered[1] * gathered[1] + gathered[2] * gathered[2] + gathered[3] * gathered[3]
@@ -311,10 +331,8 @@
     grad_low = dot_trailing(grad_pre, up_ref[...]).astype(bf16)
     grad_inv = dot_trailing(grad_pre, mix_ref[...]) + dot_trailing(grad_low, down_ref[...])
     seed = scale * grad_inv
-    cot_win[2, 0] = seed.astype(bf16)
-    for x in range(3):
-        cot_win[2, 1 + x] = (2.0 * seed * gathered[1 + x]).astype(bf16)
-    pending += cast_start(cot_win, cot_send, cot_recv)
+    agg_win[2, 0] = seed
+    pending += cast_start(agg_win, cot_send, cot_recv, (0,))
 
     rank = up_ref.shape[0]
     ring_out[0, 0:rank] = dot(jnp.transpose(grad_low.astype(f32)).astype(bf16), invariant)
@@ -342,10 +360,11 @@
         ring_out[level + 1] = ring_out[level] + ring_in[level]
 
     ring_start(0)
-    pending += cast_relay(cot_win, cot_send, cot_recv)
+    pending += cast_relay(agg_win, cot_send, cot_recv, order)
     ring_finish(0)
     ring_start(1)
-    pending += cast_finish(cot_win, cot_send, cot_recv)
+    pending += cast_forward(agg_win, cot_send, cot_recv, order)
+    cast_finish(agg_win, cot_send, cot_recv, order)
 
     lanes = lax.broadcasted_iota(jnp.int32, (atoms, atoms), 1)
     row_ids = lax.broadcasted_iota(jnp.int32, (8, atoms), 0)
@@ -355,9 +374,15 @@
         wide = jnp.concatenate([sent[j] for j in range(4)], axis=1)
         pairs = [jnp.concatenate([sent[0], sent[1 + x]], axis=1) for x in range(3)]
 
-        def gradients(k, carry, s=s, wide=wide, pairs=pairs):
-            weight = [radial_ref[path, pl.ds(k, 1), :] for path in range(4)]
-            cot = [cot_win[recv_idx[s], j].astype(f32) for j in range(4)]
+        cot = [agg_win[recv_idx[s], 0]]
+        for x in range(3):
+            cot.append(2.0 * cot[0] * agg_win[recv_idx[s], 1 + x])
+        gap = dist_buf[s]
+        units = [unit_buf[s, x] for x in range(3)]
+        grad_dist = jnp.zeros((atoms, atoms), f32)
+        dirs = [jnp.zeros((atoms, atoms), f32) for x in range(3)]
+        for k in range(basis):
+            weight = [radial_ref[path, k : k + 1, :] for path in range(4)]
             wall = jnp.concatenate(
                 [(weight[0] * cot[0]).astype(bf16)]
                 + [(weight[3] * cot[1 + x]).astype(bf16) for x in range(3)],
@@ -369,23 +394,15 @@
             for x in range(3):
                 along = (weight[2] * cot[1 + x]).astype(bf16)
                 grad_dir = dot_trailing(jnp.concatenate([along, inner], axis=1), pairs[x])
-                total = total + grad_dir * unit_buf[s, x]
-                grad_unit[x] += masked * grad_dir
-            scaled = dist_buf[s] - (centre_start + k.astype(f32))
-            grad_dist[...] += total * masked * (-2.0 * scaled)
-            return carry
-
-        grad_dist[...] = jnp.zeros(grad_dist.shape, f32)
-        grad_unit[...] = jnp.zeros(grad_unit.shape, f32)
-        lax.fori_loop(0, basis, gradients, 0)
-        units = [unit_buf[s, x] for x in range(3)]
-        dirs = [grad_unit[x] for x in range(3)]
+                total = total + grad_dir * units[x]
+                dirs[x] = dirs[x] + masked * grad_dir
+            grad_dist = grad_dist + total * masked * (-2.0 * (gap - (centre_start + k)))
         radial_part = dirs[0] * units[0] + dirs[1] * units[1] + dirs[2] * units[2]
-        inverse = 1.0 / dist_buf[s]
+        inverse = 1.0 / gap
         columns = jnp.zeros((atoms, atoms), f32)
         send_rows = jnp.zeros((8, atoms), f32)
         for x in range(3):
-            grad = grad_dist[...] * units[x] + (dirs[x] - units[x] * radial_part) * inverse
+            grad = grad_dist * units[x] + (dirs[x] - units[x] * radial_part) * inverse
             columns = jnp.where(lanes == x, jnp.sum(grad, axis=1, keepdims=True), columns)
             send_rows = jnp.where(row_ids == x, jnp.sum(grad, axis=0, keepdims=True), send_rows)
         recv_grads.append(-jnp.transpose(columns)[0:8])
@@ -420,11 +437,18 @@
             grad_out.at[w], grad_in.at[w], grad_send.at[w], grad_recv.at[w], offset(w - 2)
         ).wait_recv()
         coord = coord + grad_in[w]
-    coord_ref[...] = coord[0:3]
-    down_grad_ref[...] = jnp.transpose(ring_out[rounds, 0:rank])
-    up_grad_ref[...] = ring_out[rounds, rank:]
+    coord_ref[...] = coord
+    adapter_ref[...] = ring_out[rounds]
     for copy in pending:
         copy.wait_send()
+
+
+def finish(energy_in, coord_in, adapter_in, energy_ref, coord_ref, down_ref, up_ref):
+    rank = up_ref.shape[0]
+    energy_ref[...] = energy_in[...]
+    coord_ref[...] = coord_in[0:3]
+    down_ref[...] = jnp.transpose(adapter_in[0:rank])
+    up_ref[...] = adapter_in[rank:]
 
 
 def body(
@@ -453,34 +477,27 @@
     smem = pl.BlockSpec(memory_space=pltpu.SMEM)
     dma = pltpu.SemaphoreType.DMA
     block = (comps, atoms, channels)
-    energies, coordinate_gradient, down_gradient, up_gradient = pl.pallas_call(
+    energy_row, coord_rows, adapter_rows = pl.pallas_call(
         functools.partial(kernel, count, rounds),
         out_shape=(
             jax.ShapeDtypeStruct((1, atoms), f32),
-            jax.ShapeDtypeStruct((3, atoms), f32),
-            jax.ShapeDtypeStruct((channels, rank), f32),
-            jax.ShapeDtypeStruct((rank, channels), f32),
+            jax.ShapeDtypeStruct((8, atoms), f32),
+            jax.ShapeDtypeStruct((2 * rank, channels), f32),
         ),
         in_specs=[smem, smem] + [vmem] * 11,
-        out_specs=(vmem,) * 4,
+        out_specs=(vmem,) * 3,
         scratch_shapes=[
             pltpu.VMEM((WINDOW,) + block, bf16),
-            pltpu.VMEM((WINDOW,) + block, bf16),
+            pltpu.VMEM((WINDOW,) + block, f32),
             pltpu.VMEM((WINDOW, 8, atoms), f32),
             pltpu.VMEM((WINDOW,) + block, f32),
-            pltpu.VMEM((comps, 2, atoms, channels), f32),
-            pltpu.VMEM((comps, 2, atoms, channels), f32),
+            pltpu.VMEM((2,) + block, f32),
             pltpu.VMEM(block, f32),
             pltpu.VMEM(block, f32),
-            pltpu.VMEM(block, f32),
-            pltpu.VMEM(block, f32),
-            pltpu.VMEM((slots, basis, 4, atoms, atoms), bf16),
+            pltpu.VMEM((slots, 4, basis, atoms, atoms), bf16),
             pltpu.VMEM((slots, basis, atoms, atoms), f32),
             pltpu.VMEM((slots, atoms, atoms), f32),
             pltpu.VMEM((slots, 3, atoms, atoms), f32),
-            pltpu.VMEM((slots,) + block, f32),
-            pltpu.VMEM((atoms, atoms), f32),
-            pltpu.VMEM((3, atoms, atoms), f32),
             pltpu.VMEM((atoms, channels), f32),
             pltpu.VMEM((128, channels), f32),
             pltpu.VMEM((WINDOW, 8, atoms), f32),
@@ -493,8 +510,8 @@
             dma((WINDOW, comps)),
             dma((WINDOW,)),
             dma((WINDOW,)),
-            dma((3, comps)),
-            dma((3, comps)),
+            dma((4, comps)),
+            dma((4, comps)),
             dma((WINDOW,)),
             dma((WINDOW,)),
             dma((rounds,)),
@@ -518,6 +535,15 @@
         readout_weight.reshape(1, channels),
         atom_energy_weight.reshape(1, atoms),
     )
+    energies, coordinate_gradient, down_gradient, up_gradient = pl.pallas_call(
+        finish,
+        out_shape=(
+            jax.ShapeDtypeStruct((1, atoms), f32),
+            jax.ShapeDtypeStruct((3, atoms), f32),
+            jax.ShapeDtypeStruct((channels, rank), f32),
+            jax.ShapeDtypeStruct((rank, channels), f32),
+        ),
+    )(energy_row, coord_rows, adapter_rows)
     return (energies.reshape(atoms), coordinate_gradient, down_gradient, up_gradient)
 
 

time: 57.9 us -> 56.4 us (0.974)
  Pallas kernels: 52.1 us -> 49.7 us
  local copies, waits for them, and re-layouts: 4.15 us -> 5 us
    pallas_call x1, Pallas kernels: 52.1 us -> 48.2 us  [body(): pl.pallas_call(functools.partial(kernel, count, rounds), out_shape=(jax.S...]
    pallas_call x0 -> x1, Pallas kernels: none -> 1.46 us  [body(): pl.pallas_call(finish, out_shape=(jax.ShapeDtypeStruct((1, atoms), f32),...]
    unnamed x28 -> x31, local copies, waits for them, and re-layouts: 4.15 us -> 5 us
where the time goes in v2:
time: 56.4 us; the launch traced here: 56.1 us
  Pallas kernels  49.7 us (88%)
  local copies, waits for them, and re-layouts  5 us (9%)
  between operations  1.46 us (3%)
    pallas_call x1, Pallas kernels, body(): pl.pallas_call(functools.partial(kernel, count, rounds), out_shape=(jax.S...  48.2 us
    unnamed x31, local copies, waits for them, and re-layouts  5 us
    pallas_call x1, Pallas kernels, body(): pl.pallas_call(finish, out_shape=(jax.ShapeDtypeStruct((1, atoms), f32),...  1.46 us

profile of v2, /device:TPU:0, one launch (start us, length us, event | category | flops | bytes accessed | tf_op | source)
XLA Modules:
  0.0 56.1 jit_solution(8685757782376788075)
XLA Ops:
  0.6 0.0 copy-start.13
  1.3 0.0 copy-done.13
  1.3 0.1 copy.18.down_ref
  1.4 0.0 copy-start.1
  1.5 0.0 copy-start.2
  1.5 0.0 copy-start.3
  1.5 0.0 copy-start.5
  1.5 0.0 copy-start.7
  1.5 0.0 copy-start.10
  1.5 0.0 copy-start.11
  1.5 1.0 %copy.21 = bf16[128,4,128]{2,0,1:T(8,128)(2,1)S(1)} copy(bf16[128,4,128]{2,1,0:T(4,128)(2,1)} %param.13) | data formatting | bytes 262144 | tf_op args[0]
  2.6 0.0 copy-start.8
  2.6 0.0 copy-start.9
  2.6 0.0 copy-done
  2.6 0.0 copy-done.1
  2.6 0.0 copy-done.2
  2.6 0.0 copy-done.3
  2.7 0.6 %copy-done.8 = s32[2,2]{1,0:T(2,128)S(1)} copy-done((s32[2,2]{1,0:T(2,128)S(1)}, s32[2,2]{1,0:T(2,128)}, u32[]{:S(2)}) %copy-start.8) | copy-done | bytes 40
  3.2 48.2 %shard_map.156 = (f32[1,128]{1,0:T(1,128)S(1)}, f32[8,128]{1,0:T(8,128)S(1)}, f32[32,128]{1,0:T(8,128)S(1)}) custom-call(s32[2,2]{1,0:T(2,128)S(1)} %copy-done.8, s32[1]{0:T(128)S(6)} %copy.22.live_ref, bf16[4,128,128]{2,1,0:T(8,128)(2,1)S(1)} %bitcast.7, f32[3,128]{1,0:T(4,128)S(1)} %copy-done.7, s32[1,128]{1,0:T(1,128)S(1)} %bitcast.8, ...), custom_call_target="tpu_custom_call" | custom-call | tf_op jit(solution)/shard_map/pallas_call | solution.py:480
  51.5 0.6 %copy-done.4 = f32[32,128]{1,0:T(8,128)} copy-done((f32[32,128]{1,0:T(8,128)}, f32[32,128]{1,0:T(8,128)S(1)}, u32[]{:S(2)}) %copy-start.4) | copy-done | bytes 16408
  52.1 0.6 %copy-done.6 = f32[8,128]{1,0:T(8,128)} copy-done((f32[8,128]{1,0:T(8,128)}, f32[8,128]{1,0:T(8,128)S(1)}, u32[]{:S(2)}) %copy-start.6) | copy-done | bytes 4120
  52.6 0.5 copy-done.12
  53.2 1.5 %shard_map.157 = (f32[1,128]{1,0:T(1,128)}, f32[3,128]{1,0:T(4,128)}, f32[128,16]{1,0:T(8,128)}, f32[16,128]{1,0:T(8,128)}) custom-call(f32[1,128]{1,0:T(1,128)} %copy-done.12, f32[8,128]{1,0:T(8,128)} %copy-done.6, f32[32,128]{1,0:T(8,128)} %copy-done.4), custom_call_target="tpu_custom_call" | custom-call | tf_op jit(solution)/shard_map/pallas_call | solution.py:538
  54.6 1.5 %copy.19 = f32[128,16]{0,1:T(8,128)} copy(f32[128,16]{1,0:T(8,128)} %get-tuple-element.20) | data formatting | bytes 16384
  (9 shorter events, 0.0 us)
Async XLA Ops:
  0.6 0.7 %copy-start.13 = (bf16[128,16]{0,1:T(8,128)(2,1)S(1)}, bf16[128,16]{0,1:T(8,128)(2,1)}, u32[]{:S(2)}) copy-start(bf16[128,16]{0,1:T(8,128)(2,1)} %param.22) | copy-start | bytes 12292
  1.4 1.1 %copy-start = (s32[2,128,128]{2,1,0:T(8,128)S(1)}, s32[2,128,128]{2,1,0:T(8,128)}, u32[]{:S(2)}) copy-start(s32[2,128,128]{2,1,0:T(8,128)} %mask_ref.1) | copy-start | bytes 393220
  1.4 1.1 %copy-start.1 = (f32[89,128]{1,0:T(8,128)S(1)}, f32[89,128]{1,0:T(8,128)}, u32[]{:S(2)}) copy-start(f32[89,128]{1,0:T(8,128)} %scale_ref.1) | copy-start | bytes 136708
  1.5 1.1 %copy-start.2 = (bf16[128,128]{1,0:T(8,128)(2,1)S(1)}, bf16[128,128]{1,0:T(8,128)(2,1)}, u32[]{:S(2)}) copy-start(bf16[128,128]{1,0:T(8,128)(2,1)} %mix_ref.1) | copy-start | bytes 98308
  1.5 1.1 %copy-start.3 = (f32[4,8,128]{2,1,0:T(8,128)S(1)}, f32[4,8,128]{2,1,0:T(8,128)}, u32[]{:S(2)}) copy-start(f32[4,8,128]{2,1,0:T(8,128)} %radial_ref.1) | copy-start | bytes 49156
  1.5 1.1 %copy-start.5 = (bf16[16,128]{1,0:T(8,128)(2,1)S(1)}, bf16[16,128]{1,0:T(8,128)(2,1)}, u32[]{:S(2)}) copy-start(bf16[16,128]{1,0:T(8,128)(2,1)} %up_ref.1) | copy-start | bytes 12292
  1.5 1.1 %copy-start.7 = (f32[3,128]{1,0:T(4,128)S(1)}, f32[3,128]{1,0:T(4,128)}, u32[]{:S(2)}) copy-start(f32[3,128]{1,0:T(4,128)} %pos_ref.1) | copy-start | bytes 4612
  1.5 1.1 %copy-start.10 = (f32[128]{0:T(128)S(1)}, f32[128]{0:T(128)}, u32[]{:S(2)}) copy-start(f32[128]{0:T(128)} %param.24) | copy-start | bytes 1540
  1.5 1.1 %copy-start.11 = (f32[128]{0:T(128)S(1)}, f32[128]{0:T(128)}, u32[]{:S(2)}) copy-start(f32[128]{0:T(128)} %param.25) | copy-start | bytes 1540
  2.6 0.7 %copy-start.8 = (s32[2,2]{1,0:T(2,128)S(1)}, s32[2,2]{1,0:T(2,128)}, u32[]{:S(2)}) copy-start(s32[2,2]{1,0:T(2,128)} %table_ref.1) | copy-start | bytes 52
  2.6 0.7 %copy-start.9 = (s32[128]{0:T(128)S(1)}, s32[128]{0:T(128)}, u32[]{:S(2)}) copy-start(s32[128]{0:T(128)} %param.15) | copy-start | bytes 1540
  51.5 0.6 %copy-start.4 = (f32[32,128]{1,0:T(8,128)}, f32[32,128]{1,0:T(8,128)S(1)}, u32[]{:S(2)}) copy-start(f32[32,128]{1,0:T(8,128)S(1)} %get-tuple-element.13.adapter_in) | copy-start | bytes 49156
  52.0 0.6 %copy-start.6 = (f32[8,128]{1,0:T(8,128)}, f32[8,128]{1,0:T(8,128)S(1)}, u32[]{:S(2)}) copy-start(f32[8,128]{1,0:T(8,128)S(1)} %get-tuple-element.12.coord_in) | copy-start | bytes 12292
  52.6 0.5 copy-start.12

commit v3 on v2

--- a/solution.py
+++ b/solution.py
@@ -14,6 +14,9 @@
 centre_start = 1.0
 highest = lax.Precision.HIGHEST
 MESH = pl.DeviceIdType.MESH
+FEAT_DIRECT = (0, 1, 2, 3)
+MSG_DIRECT = (0,)
+COT_DIRECT = (0,)
 f32 = jnp.float32
 bf16 = jnp.bfloat16
 
@@ -45,8 +48,14 @@
     energy_ref,
     coord_ref,
     adapter_ref,
-    feat_win,
-    agg_win,
+    feat_0,
+    feat_1,
+    feat_2,
+    feat_3,
+    agg_0,
+    agg_1,
+    agg_2,
+    agg_3,
     pos_win,
     partial,
     sib_in,
@@ -76,6 +85,8 @@
     ring_recv,
 ):
     comps, atoms, channels = feat_ref.shape
+    feat_win = (feat_0, feat_1, feat_2, feat_3)
+    agg_win = (agg_0, agg_1, agg_2, agg_3)
     slots = mask_ref.shape[0]
     basis = radial_ref.shape[1]
     me = lax.axis_index("space")
@@ -83,6 +94,7 @@
     col = lax.rem(me // 2, 2)
     sib = me + 1 - 2 * core
     near = me + 2 - 4 * col
+    far = lax.rem(me - 2 + 4 * col + count, count)
     onward = lax.rem(me + 4 - 8 * col + count, count)
     behind = lax.rem(me - 4 + 8 * col + count, count)
     near_slot = 4 - 4 * col
@@ -114,7 +126,8 @@
     for device in greeted:
         pl.semaphore_signal(barrier, inc=1, device_id={"space": device}, device_id_type=MESH)
 
-    feat_win[2] = feat_ref[...]
+    for j in range(comps):
+        feat_win[j][2] = feat_ref[j]
     pos_win[2] = jnp.zeros(pos_win.shape[1:], f32)
     pos_win[2, 0:3] = pos_ref[...]
     table_pad[...] = jnp.zeros(table_pad.shape, f32)
@@ -122,50 +135,48 @@
 
     pl.semaphore_wait(barrier, len(greeted))
 
-    def cast_start(win, send, recv, parts):
-        copies = []
-        for target, slot, kind in ((near, far_slot, 0), (sib, oth_slot, 1)):
-            for j in parts:
-                copies.append(
-                    remote(win.at[2, j], win.at[slot, j], send.at[kind, j], recv.at[slot, j], target)
-                )
-                copies[-1].start()
-        return copies
+    def cast_copy(win, send, recv, kind, j):
+        src, dst, device = (
+            (2, far_slot, near),
+            (2, oth_slot, sib),
+            (near_slot, far_slot, onward),
+            (through_slot, sib_slot, sib),
+            (2, near_slot, far),
+        )[kind]
+        return remote(
+            win[j].at[src], win[j].at[dst], send.at[kind, j], recv.at[dst, j], device
+        )
+
+    def cast_begin(win, send, recv, kind, j):
+        copy = cast_copy(win, send, recv, kind, j)
+        copy.start()
+        pending.append(copy)
+
+    def cast_start(win, send, recv, parts, direct):
+        for j in parts:
+            cast_begin(win, send, recv, 0, j)
+            if j in direct:
+                cast_begin(win, send, recv, 4, j)
+        for j in parts:
+            cast_begin(win, send, recv, 1, j)
 
     def arrived(win, send, recv, slot, j):
-        remote(win.at[2, j], win.at[slot, j], send.at[0, j], recv.at[slot, j], near).wait_recv()
-
-    def cast_relay(win, send, recv, parts):
-        copies = []
+        remote(
+            win[j].at[2], win[j].at[slot], send.at[0, j], recv.at[slot, j], near
+        ).wait_recv()
+
+    def cast_relay(win, send, recv, parts, direct):
         for j in parts:
-            arrived(win, send, recv, near_slot, j)
-            copies.append(
-                remote(
-                    win.at[near_slot, j],
-                    win.at[far_slot, j],
-                    send.at[2, j],
-                    recv.at[far_slot, j],
-                    onward,
-                )
-            )
-            copies[-1].start()
-        return copies
-
-    def cast_forward(win, send, recv, parts):
-        copies = []
+            if j not in direct:
+                arrived(win, send, recv, near_slot, j)
+                cast_begin(win, send, recv, 2, j)
+
+    def cast_forward(win, send, recv, parts, direct):
         for j in parts:
+            if j in direct:
+                arrived(win, send, recv, near_slot, j)
             arrived(win, send, recv, far_slot, j)
-            copies.append(
-                remote(
-                    win.at[through_slot, j],
-                    win.at[sib_slot, j],
-                    send.at[3, j],
-                    recv.at[sib_slot, j],
-                    sib,
-                )
-            )
-            copies[-1].start()
-        return copies
+            cast_begin(win, send, recv, 3, j)
 
     def cast_finish(win, send, recv, parts):
         for j in parts:
@@ -173,6 +184,8 @@
             arrived(win, send, recv, oth_slot, j)
 
     order = (1, 2, 3, 0)
+    feat = (feat_win, feat_send, feat_recv)
+    agg = (agg_win, cot_send, cot_recv)
     pending = []
     pos_copies = []
     for w in (0, 1, 3, 4):
@@ -185,7 +198,7 @@
         )
         copy.start()
         pos_copies.append(copy)
-    pending += cast_start(feat_win, feat_send, feat_recv, range(comps))
+    cast_start(*feat, range(comps), FEAT_DIRECT)
 
     species_cols = lax.broadcasted_iota(jnp.int32, (atoms, atoms), 0) == species_ref[...]
     one_hot = jnp.transpose(species_cols.astype(f32))
@@ -207,7 +220,7 @@
             pos_win.at[2], pos_win.at[w], pos_send.at[w], pos_recv.at[w], offset(w - 2)
         ).wait_recv()
 
-    pending += cast_relay(feat_win, feat_send, feat_recv, range(comps))
+    cast_relay(*feat, range(comps), FEAT_DIRECT)
 
     for s in range(slots):
         columns = jnp.transpose(pos_win[recv_idx[s]])
@@ -232,8 +245,8 @@
 
         lax.fori_loop(0, basis, build, 0)
 
-    pending += cast_forward(feat_win, feat_send, feat_recv, range(comps))
-    cast_finish(feat_win, feat_send, feat_recv, range(comps))
+    cast_forward(*feat, (0, 1), FEAT_DIRECT)
+    cast_finish(*feat, (0, 1))
 
     share = [
         [jnp.where(recv_idx[s] == w, live[s], 0.0) for s in range(slots)] for w in range(WINDOW)
@@ -249,15 +262,15 @@
         terms = []
         for s in range(slots):
             plain = lefts[s, 0].reshape(basis * atoms, atoms)
-            straight = dot(plain, feat_win[send_idx[s], j])
+            straight = dot(plain, feat_win[j][send_idx[s]])
             if j == 0:
                 turned = [lefts[s, 1 + x].reshape(basis * atoms, atoms) for x in range(3)]
-                tall = feat_win[send_idx[s]][1:].reshape(3 * atoms, channels)
+                tall = jnp.concatenate([feat_win[1 + x][send_idx[s]] for x in range(3)], axis=0)
                 crossed = dot(jnp.concatenate(turned, axis=1), tall)
                 terms.append(weighted(straight, 0) + weighted(crossed, 1))
             else:
                 turned = lefts[s, j].reshape(basis * atoms, atoms)
-                crossed = dot(turned, feat_win[send_idx[s], 0])
+                crossed = dot(turned, feat_win[0][send_idx[s]])
                 terms.append(weighted(crossed, 2) + weighted(straight, 3))
         for w in range(WINDOW):
             total = share[w][0] * terms[0]
@@ -269,7 +282,7 @@
         src, dst, device = (
             (partial.at[oth_slot, j], sib_in.at[0, j], sib),
             (partial.at[sib_slot, j], sib_in.at[1, j], sib),
-            (partial.at[far_slot, j], far_in.at[j], behind),
+            (partial.at[far_slot, j], far_in.at[j], far if j in MSG_DIRECT else behind),
             (partial.at[near_slot, j], near_in.at[j], near),
         )[hop]
         return remote(src, dst, msg_send.at[hop, j], msg_recv.at[hop, j], device)
@@ -290,32 +303,44 @@
         message_start(2, j)
 
     def to_near(j):
-        message_copy(2, j).wait_recv()
-        partial[near_slot, j] += far_in[j]
+        if j not in MSG_DIRECT:
+            message_copy(2, j).wait_recv()
+            partial[near_slot, j] += far_in[j]
         message_start(3, j)
 
     def gather(j):
         message_copy(1, j).wait_recv()
+        total = partial[2, j] + sib_in[1, j]
+        if j in MSG_DIRECT:
+            message_copy(2, j).wait_recv()
+            total = total + far_in[j]
         message_copy(3, j).wait_recv()
-        return partial[2, j] + sib_in[1, j] + near_in[j]
+        return total + near_in[j]
 
     to_sib(1)
+    cast_forward(*feat, (2,), FEAT_DIRECT)
+    cast_finish(*feat, (2,))
     to_sib(2)
     to_far(1)
+    cast_forward(*feat, (3,), FEAT_DIRECT)
+    cast_finish(*feat, (3,))
     to_sib(3)
     to_far(2)
     to_sib(0)
     to_near(1)
     to_far(3)
     to_far(0)
+    if 0 in MSG_DIRECT:
+        to_near(0)
     to_near(2)
     to_near(3)
+    if 0 not in MSG_DIRECT:
+        to_near(0)
     for j in (1, 2, 3):
-        agg_win[2, j] = gather(j)
-        pending += cast_start(agg_win, cot_send, cot_recv, (j,))
-        if j == 1:
-            to_near(0)
-    gathered = [gather(0)] + [agg_win[2, j] for j in (1, 2, 3)]
+        agg_win[j][2] = gather(j)
+        cast_start(*agg, (j,), COT_DIRECT)
+    cast_relay(*agg, (1, 2), COT_DIRECT)
+    gathered = [gather(0)] + [agg_win[j][2] for j in (1, 2, 3)]
 
     scale = scale_buf[...]
     squares = gathered[1] * gathered[1] + gathered[2] * gathered[2] + gathered[3] * gathered[3]
@@ -331,8 +356,9 @@
     grad_low = dot_trailing(grad_pre, up_ref[...]).astype(bf16)
     grad_inv = dot_trailing(grad_pre, mix_ref[...]) + dot_trailing(grad_low, down_ref[...])
     seed = scale * grad_inv
-    agg_win[2, 0] = seed
-    pending += cast_start(agg_win, cot_send, cot_recv, (0,))
+    agg_win[0][2] = seed
+    cast_start(*agg, (0,), COT_DIRECT)
+    cast_relay(*agg, (3, 0), COT_DIRECT)
 
     rank = up_ref.shape[0]
     ring_out[0, 0:rank] = dot(jnp.transpose(grad_low.astype(f32)).astype(bf16), invariant)
@@ -360,23 +386,22 @@
         ring_out[level + 1] = ring_out[level] + ring_in[level]
 
     ring_start(0)
-    pending += cast_relay(agg_win, cot_send, cot_recv, order)
     ring_finish(0)
     ring_start(1)
-    pending += cast_forward(agg_win, cot_send, cot_recv, order)
-    cast_finish(agg_win, cot_send, cot_recv, order)
+    cast_forward(*agg, order, COT_DIRECT)
+    cast_finish(*agg, order)
 
     lanes = lax.broadcasted_iota(jnp.int32, (atoms, atoms), 1)
     row_ids = lax.broadcasted_iota(jnp.int32, (8, atoms), 0)
     recv_grads, send_grads = [], []
     for s in range(slots):
-        sent = feat_win[send_idx[s]]
-        wide = jnp.concatenate([sent[j] for j in range(4)], axis=1)
+        sent = [feat_win[j][send_idx[s]] for j in range(4)]
+        wide = jnp.concatenate(sent, axis=1)
         pairs = [jnp.concatenate([sent[0], sent[1 + x]], axis=1) for x in range(3)]
 
-        cot = [agg_win[recv_idx[s], 0]]
+        cot = [agg_win[0][recv_idx[s]]]
         for x in range(3):
-            cot.append(2.0 * cot[0] * agg_win[recv_idx[s], 1 + x])
+            cot.append(2.0 * cot[0] * agg_win[1 + x][recv_idx[s]])
         gap = dist_buf[s]
         units = [unit_buf[s, x] for x in range(3)]
         grad_dist = jnp.zeros((atoms, atoms), f32)
@@ -487,8 +512,8 @@
         in_specs=[smem, smem] + [vmem] * 11,
         out_specs=(vmem,) * 3,
         scratch_shapes=[
-            pltpu.VMEM((WINDOW,) + block, bf16),
-            pltpu.VMEM((WINDOW,) + block, f32),
+            *[pltpu.VMEM((WINDOW, atoms, channels), bf16)] * comps,
+            *[pltpu.VMEM((WINDOW, atoms, channels), f32)] * comps,
             pltpu.VMEM((WINDOW, 8, atoms), f32),
             pltpu.VMEM((WINDOW,) + block, f32),
             pltpu.VMEM((2,) + block, f32),
@@ -504,9 +529,9 @@
             pltpu.VMEM((WINDOW, 8, atoms), f32),
             pltpu.VMEM((rounds + 1, 2 * rank, channels), f32),
             pltpu.VMEM((rounds, 2 * rank, channels), f32),
-            dma((4, comps)),
+            dma((5, comps)),
             dma((WINDOW, comps)),
-            dma((4, comps)),
+            dma((5, comps)),
             dma((WINDOW, comps)),
             dma((WINDOW,)),
             dma((WINDOW,)),

time: 56.4 us -> 53.3 us (0.945)
  Pallas kernels: 49.7 us -> 46.5 us
    pallas_call x1, Pallas kernels: 48.2 us -> 45.1 us  [body(): pl.pallas_call(functools.partial(kernel, count, rounds), out_shape=(jax.S...]
where the time goes in v3:
time: 53.3 us; the launch traced here: 53 us
  Pallas kernels  46.5 us (87%)
  local copies, waits for them, and re-layouts  5 us (9%)
  between operations  1.46 us (3%)
    pallas_call x1, Pallas kernels, body(): pl.pallas_call(functools.partial(kernel, count, rounds), out_shape=(jax.S...  45.1 us
    unnamed x31, local copies, waits for them, and re-layouts  5 us
    pallas_call x1, Pallas kernels, body(): pl.pallas_call(finish, out_shape=(jax.ShapeDtypeStruct((1, atoms), f32),...  1.46 us

profile of v3, /device:TPU:0, one launch (start us, length us, event | category | flops | bytes accessed | tf_op | source)
XLA Modules:
  0.0 53.0 jit_solution(5551094417958231724)
XLA Ops:
  0.6 0.0 copy-start.13
  1.3 0.0 copy-done.13
  1.3 0.1 copy.18.down_ref
  1.4 0.0 copy-start.1
  1.5 0.0 copy-start.2
  1.5 0.0 copy-start.3
  1.5 0.0 copy-start.5
  1.5 0.0 copy-start.7
  1.5 0.0 copy-start.10
  1.5 0.0 copy-start.11
  1.5 1.0 %copy.21 = bf16[128,4,128]{2,0,1:T(8,128)(2,1)S(1)} copy(bf16[128,4,128]{2,1,0:T(4,128)(2,1)} %param.13) | data formatting | bytes 262144 | tf_op args[0]
  2.6 0.0 copy-start.8
  2.6 0.0 copy-start.9
  2.6 0.0 copy-done
  2.6 0.0 copy-done.1
  2.6 0.0 copy-done.2
  2.6 0.0 copy-done.3
  2.7 0.6 %copy-done.8 = s32[2,2]{1,0:T(2,128)S(1)} copy-done((s32[2,2]{1,0:T(2,128)S(1)}, s32[2,2]{1,0:T(2,128)}, u32[]{:S(2)}) %copy-start.8) | copy-done | bytes 40
  3.2 45.1 %shard_map.156 = (f32[1,128]{1,0:T(1,128)S(1)}, f32[8,128]{1,0:T(8,128)S(1)}, f32[32,128]{1,0:T(8,128)S(1)}) custom-call(s32[2,2]{1,0:T(2,128)S(1)} %copy-done.8, s32[1]{0:T(128)S(6)} %copy.22.live_ref, bf16[4,128,128]{2,1,0:T(8,128)(2,1)S(1)} %bitcast.7, f32[3,128]{1,0:T(4,128)S(1)} %copy-done.7, s32[1,128]{1,0:T(1,128)S(1)} %bitcast.8, ...), custom_call_target="tpu_custom_call" | custom-call | tf_op jit(solution)/shard_map/pallas_call | solution.py:505
  48.3 0.6 %copy-done.4 = f32[32,128]{1,0:T(8,128)} copy-done((f32[32,128]{1,0:T(8,128)}, f32[32,128]{1,0:T(8,128)S(1)}, u32[]{:S(2)}) %copy-start.4) | copy-done | bytes 16408
  48.9 0.6 %copy-done.6 = f32[8,128]{1,0:T(8,128)} copy-done((f32[8,128]{1,0:T(8,128)}, f32[8,128]{1,0:T(8,128)S(1)}, u32[]{:S(2)}) %copy-start.6) | copy-done | bytes 4120
  49.5 0.5 copy-done.12
  50.0 1.5 %shard_map.157 = (f32[1,128]{1,0:T(1,128)}, f32[3,128]{1,0:T(4,128)}, f32[128,16]{1,0:T(8,128)}, f32[16,128]{1,0:T(8,128)}) custom-call(f32[1,128]{1,0:T(1,128)} %copy-done.12, f32[8,128]{1,0:T(8,128)} %copy-done.6, f32[32,128]{1,0:T(8,128)} %copy-done.4), custom_call_target="tpu_custom_call" | custom-call | tf_op jit(solution)/shard_map/pallas_call | solution.py:563
  51.5 1.5 %copy.19 = f32[128,16]{0,1:T(8,128)} copy(f32[128,16]{1,0:T(8,128)} %get-tuple-element.20) | data formatting | bytes 16384
  (9 shorter events, 0.0 us)
Async XLA Ops:
  0.6 0.7 %copy-start.13 = (bf16[128,16]{0,1:T(8,128)(2,1)S(1)}, bf16[128,16]{0,1:T(8,128)(2,1)}, u32[]{:S(2)}) copy-start(bf16[128,16]{0,1:T(8,128)(2,1)} %param.22) | copy-start | bytes 12292
  1.4 1.1 %copy-start = (s32[2,128,128]{2,1,0:T(8,128)S(1)}, s32[2,128,128]{2,1,0:T(8,128)}, u32[]{:S(2)}) copy-start(s32[2,128,128]{2,1,0:T(8,128)} %mask_ref.1) | copy-start | bytes 393220
  1.4 1.1 %copy-start.1 = (f32[89,128]{1,0:T(8,128)S(1)}, f32[89,128]{1,0:T(8,128)}, u32[]{:S(2)}) copy-start(f32[89,128]{1,0:T(8,128)} %scale_ref.1) | copy-start | bytes 136708
  1.5 1.1 %copy-start.2 = (bf16[128,128]{1,0:T(8,128)(2,1)S(1)}, bf16[128,128]{1,0:T(8,128)(2,1)}, u32[]{:S(2)}) copy-start(bf16[128,128]{1,0:T(8,128)(2,1)} %mix_ref.1) | copy-start | bytes 98308
  1.5 1.1 %copy-start.3 = (f32[4,8,128]{2,1,0:T(8,128)S(1)}, f32[4,8,128]{2,1,0:T(8,128)}, u32[]{:S(2)}) copy-start(f32[4,8,128]{2,1,0:T(8,128)} %radial_ref.1) | copy-start | bytes 49156
  1.5 1.1 %copy-start.5 = (bf16[16,128]{1,0:T(8,128)(2,1)S(1)}, bf16[16,128]{1,0:T(8,128)(2,1)}, u32[]{:S(2)}) copy-start(bf16[16,128]{1,0:T(8,128)(2,1)} %up_ref.1) | copy-start | bytes 12292
  1.5 1.1 %copy-start.7 = (f32[3,128]{1,0:T(4,128)S(1)}, f32[3,128]{1,0:T(4,128)}, u32[]{:S(2)}) copy-start(f32[3,128]{1,0:T(4,128)} %pos_ref.1) | copy-start | bytes 4612
  1.5 1.1 %copy-start.10 = (f32[128]{0:T(128)S(1)}, f32[128]{0:T(128)}, u32[]{:S(2)}) copy-start(f32[128]{0:T(128)} %param.24) | copy-start | bytes 1540
  1.5 1.1 %copy-start.11 = (f32[128]{0:T(128)S(1)}, f32[128]{0:T(128)}, u32[]{:S(2)}) copy-start(f32[128]{0:T(128)} %param.25) | copy-start | bytes 1540
  2.6 0.7 %copy-start.8 = (s32[2,2]{1,0:T(2,128)S(1)}, s32[2,2]{1,0:T(2,128)}, u32[]{:S(2)}) copy-start(s32[2,2]{1,0:T(2,128)} %table_ref.1) | copy-start | bytes 52
  2.6 0.7 %copy-start.9 = (s32[128]{0:T(128)S(1)}, s32[128]{0:T(128)}, u32[]{:S(2)}) copy-start(s32[128]{0:T(128)} %param.15) | copy-start | bytes 1540
  48.3 0.6 %copy-start.4 = (f32[32,128]{1,0:T(8,128)}, f32[32,128]{1,0:T(8,128)S(1)}, u32[]{:S(2)}) copy-start(f32[32,128]{1,0:T(8,128)S(1)} %get-tuple-element.13.adapter_in) | copy-start | bytes 49156
  48.9 0.6 %copy-start.6 = (f32[8,128]{1,0:T(8,128)}, f32[8,128]{1,0:T(8,128)S(1)}, u32[]{:S(2)}) copy-start(f32[8,128]{1,0:T(8,128)S(1)} %get-tuple-element.12.coord_in) | copy-start | bytes 12292
  49.5 0.5 copy-start.12

commit v4 on v3

--- a/solution.py
+++ b/solution.py
@@ -47,7 +47,8 @@
     weight_ref,
     energy_ref,
     coord_ref,
-    adapter_ref,
+    down_grad_ref,
+    up_grad_ref,
     feat_0,
     feat_1,
     feat_2,
@@ -187,7 +188,6 @@
     feat = (feat_win, feat_send, feat_recv)
     agg = (agg_win, cot_send, cot_recv)
     pending = []
-    pos_copies = []
     for w in (0, 1, 3, 4):
         copy = remote(
             pos_win.at[2],
@@ -197,7 +197,7 @@
             offset(w - 2),
         )
         copy.start()
-        pos_copies.append(copy)
+        pending.append(copy)
     cast_start(*feat, range(comps), FEAT_DIRECT)
 
     species_cols = lax.broadcasted_iota(jnp.int32, (atoms, atoms), 0) == species_ref[...]
@@ -213,8 +213,6 @@
     send_idx = [window_of(table_ref[1, s]) for s in range(slots)]
     live = [jnp.where(s < live_ref[0], 1.0, 0.0).astype(f32) for s in range(slots)]
 
-    for copy in pos_copies:
-        copy.wait_send()
     for w in (0, 1, 3, 4):
         remote(
             pos_win.at[2], pos_win.at[w], pos_send.at[w], pos_recv.at[w], offset(w - 2)
@@ -339,7 +337,7 @@
     for j in (1, 2, 3):
         agg_win[j][2] = gather(j)
         cast_start(*agg, (j,), COT_DIRECT)
-    cast_relay(*agg, (1, 2), COT_DIRECT)
+    cast_relay(*agg, (1,), COT_DIRECT)
     gathered = [gather(0)] + [agg_win[j][2] for j in (1, 2, 3)]
 
     scale = scale_buf[...]
@@ -358,7 +356,7 @@
     seed = scale * grad_inv
     agg_win[0][2] = seed
     cast_start(*agg, (0,), COT_DIRECT)
-    cast_relay(*agg, (3, 0), COT_DIRECT)
+    cast_relay(*agg, (2, 3, 0), COT_DIRECT)
 
     rank = up_ref.shape[0]
     ring_out[0, 0:rank] = dot(jnp.transpose(grad_low.astype(f32)).astype(bf16), invariant)
@@ -462,18 +460,11 @@
             grad_out.at[w], grad_in.at[w], grad_send.at[w], grad_recv.at[w], offset(w - 2)
         ).wait_recv()
         coord = coord + grad_in[w]
-    coord_ref[...] = coord
-    adapter_ref[...] = ring_out[rounds]
+    coord_ref[...] = coord[0:3]
+    down_grad_ref[...] = ring_out[rounds, 0:rank]
+    up_grad_ref[...] = ring_out[rounds, rank:]
     for copy in pending:
         copy.wait_send()
-
-
-def finish(energy_in, coord_in, adapter_in, energy_ref, coord_ref, down_ref, up_ref):
-    rank = up_ref.shape[0]
-    energy_ref[...] = energy_in[...]
-    coord_ref[...] = coord_in[0:3]
-    down_ref[...] = jnp.transpose(adapter_in[0:rank])
-    up_ref[...] = adapter_in[rank:]
 
 
 def body(
@@ -502,15 +493,16 @@
     smem = pl.BlockSpec(memory_space=pltpu.SMEM)
     dma = pltpu.SemaphoreType.DMA
     block = (comps, atoms, channels)
-    energy_row, coord_rows, adapter_rows = pl.pallas_call(
+    energies, coordinate_gradient, down_gradient, up_gradient = pl.pallas_call(
         functools.partial(kernel, count, rounds),
         out_shape=(
             jax.ShapeDtypeStruct((1, atoms), f32),
-            jax.ShapeDtypeStruct((8, atoms), f32),
-            jax.ShapeDtypeStruct((2 * rank, channels), f32),
+            jax.ShapeDtypeStruct((3, atoms), f32),
+            jax.ShapeDtypeStruct((rank, channels), f32),
+            jax.ShapeDtypeStruct((rank, channels), f32),
         ),
         in_specs=[smem, smem] + [vmem] * 11,
-        out_specs=(vmem,) * 3,
+        out_specs=(vmem,) * 4,
         scratch_shapes=[
             *[pltpu.VMEM((WINDOW, atoms, channels), bf16)] * comps,
             *[pltpu.VMEM((WINDOW, atoms, channels), f32)] * comps,
@@ -560,16 +552,12 @@
         readout_weight.reshape(1, channels),
         atom_energy_weight.reshape(1, atoms),
     )
-    energies, coordinate_gradient, down_gradient, up_gradient = pl.pallas_call(
-        finish,
-        out_shape=(
-            jax.ShapeDtypeStruct((1, atoms), f32),
-            jax.ShapeDtypeStruct((3, atoms), f32),
-            jax.ShapeDtypeStruct((channels, rank), f32),
-            jax.ShapeDtypeStruct((rank, channels), f32),
-        ),
-    )(energy_row, coord_rows, adapter_rows)
-    return (energies.reshape(atoms), coordinate_gradient, down_gradient, up_gradient)
+    return (
+        energies.reshape(atoms),
+        coordinate_gradient,
+        jnp.transpose(down_gradient),
+        up_gradient,
+    )
 
 
 def solution(mesh):

time: 53.3 us -> 50.8 us (0.953)
  Pallas kernels: 46.5 us -> 45 us
  local copies, waits for them, and re-layouts: 5 us -> 4.08 us
    pallas_call x1 -> x0, Pallas kernels: 1.46 us -> none  [body(): pl.pallas_call(finish, out_shape=(jax.ShapeDtypeStruct((1, atoms), f32),...]
    unnamed x31 -> x28, local copies, waits for them, and re-layouts: 5 us -> 4.08 us
where the time goes in v4:
time: 50.8 us; the launch traced here: 50.6 us
  Pallas kernels  45 us (89%)
  local copies, waits for them, and re-layouts  4.08 us (8%)
  between operations  1.45 us (3%)
    pallas_call x1, Pallas kernels, body(): pl.pallas_call(functools.partial(kernel, count, rounds), out_shape=(jax.S...  45 us
    unnamed x28, local copies, waits for them, and re-layouts  4.08 us

profile of v4, /device:TPU:0, one launch (start us, length us, event | category | flops | bytes accessed | tf_op | source)
XLA Modules:
  0.0 50.6 jit_solution(13671729768526448388)
XLA Ops:
  0.6 0.0 copy-start.10
  1.3 0.0 copy-done.10
  1.3 0.1 copy.18.down_ref
  1.4 0.0 copy-start.1
  1.5 0.0 copy-start.2
  1.5 0.0 copy-start.3
  1.5 0.0 copy-start.4
  1.5 0.0 copy-start.5
  1.5 0.0 copy-start.8
  1.5 0.0 copy-start.9
  1.5 1.0 %copy.20 = bf16[128,4,128]{2,0,1:T(8,128)(2,1)S(1)} copy(bf16[128,4,128]{2,1,0:T(4,128)(2,1)} %param.13) | data formatting | bytes 262144 | tf_op args[0]
  2.6 0.0 copy-start.6
  2.6 0.0 copy-start.7
  2.6 0.0 copy-done
  2.6 0.0 copy-done.1
  2.6 0.0 copy-done.2
  2.6 0.0 copy-done.3
  2.6 0.0 copy-done.4
  2.7 0.6 %copy-done.6 = s32[2,2]{1,0:T(2,128)S(1)} copy-done((s32[2,2]{1,0:T(2,128)S(1)}, s32[2,2]{1,0:T(2,128)}, u32[]{:S(2)}) %copy-start.6) | copy-done | bytes 40
  3.2 45.0 %shard_map.156 = (f32[1,128]{1,0:T(1,128)S(1)}, f32[3,128]{1,0:T(4,128)S(1)}, f32[16,128]{1,0:T(8,128)S(1)}, f32[16,128]{1,0:T(8,128)S(1)}) custom-call(s32[2,2]{1,0:T(2,128)S(1)} %copy-done.6, s32[1]{0:T(128)S(6)} %copy.25.live_ref, bf16[4,128,128]{2,1,0:T(8,128)(2,1)S(1)} %bitcast.8, f32[3,128]{1,0:T(4,128)S(1)} %copy-done.5, s32[1,128]{1,0:T(1,128)S(1)} %bitcast.10, ...), custom_call_target="tpu_custom_call" | custom-call | tf_op jit(solution)/shard_map/pallas_call | solution.py:496
  48.3 0.5 %copy.26 = f32[128]{0:T(128)} copy(f32[128]{0:T(128)S(1)} %bitcast.13) | data formatting | bytes 1024
  48.8 0.6 %copy.27 = f32[3,128]{1,0:T(4,128)} copy(f32[3,128]{1,0:T(4,128)S(1)} %get-tuple-element.17) | data formatting | bytes 3072
  49.4 0.6 %copy.28 = f32[128,16]{0,1:T(8,128)} copy(f32[128,16]{0,1:T(8,128)S(1)} %bitcast.9) | data formatting | bytes 16384
  50.0 0.6 %copy.29 = f32[16,128]{1,0:T(8,128)} copy(f32[16,128]{1,0:T(8,128)S(1)} %get-tuple-element.19) | data formatting | bytes 16384
  (5 shorter events, 0.0 us)
Async XLA Ops:
  0.6 0.7 %copy-start.10 = (bf16[128,16]{0,1:T(8,128)(2,1)S(1)}, bf16[128,16]{0,1:T(8,128)(2,1)}, u32[]{:S(2)}) copy-start(bf16[128,16]{0,1:T(8,128)(2,1)} %param.22) | copy-start | bytes 12292
  1.4 1.1 %copy-start = (s32[2,128,128]{2,1,0:T(8,128)S(1)}, s32[2,128,128]{2,1,0:T(8,128)}, u32[]{:S(2)}) copy-start(s32[2,128,128]{2,1,0:T(8,128)} %mask_ref.1) | copy-start | bytes 393220
  1.4 1.1 %copy-start.1 = (f32[89,128]{1,0:T(8,128)S(1)}, f32[89,128]{1,0:T(8,128)}, u32[]{:S(2)}) copy-start(f32[89,128]{1,0:T(8,128)} %scale_ref.1) | copy-start | bytes 136708
  1.5 1.1 %copy-start.2 = (bf16[128,128]{1,0:T(8,128)(2,1)S(1)}, bf16[128,128]{1,0:T(8,128)(2,1)}, u32[]{:S(2)}) copy-start(bf16[128,128]{1,0:T(8,128)(2,1)} %mix_ref.1) | copy-start | bytes 98308
  1.5 1.1 %copy-start.3 = (f32[4,8,128]{2,1,0:T(8,128)S(1)}, f32[4,8,128]{2,1,0:T(8,128)}, u32[]{:S(2)}) copy-start(f32[4,8,128]{2,1,0:T(8,128)} %radial_ref.1) | copy-start | bytes 49156
  1.5 1.1 %copy-start.4 = (bf16[16,128]{1,0:T(8,128)(2,1)S(1)}, bf16[16,128]{1,0:T(8,128)(2,1)}, u32[]{:S(2)}) copy-start(bf16[16,128]{1,0:T(8,128)(2,1)} %up_ref.1) | copy-start | bytes 12292
  1.5 1.1 %copy-start.5 = (f32[3,128]{1,0:T(4,128)S(1)}, f32[3,128]{1,0:T(4,128)}, u32[]{:S(2)}) copy-start(f32[3,128]{1,0:T(4,128)} %pos_ref.1) | copy-start | bytes 4612
  1.5 1.1 %copy-start.8 = (f32[128]{0:T(128)S(1)}, f32[128]{0:T(128)}, u32[]{:S(2)}) copy-start(f32[128]{0:T(128)} %param.24) | copy-start | bytes 1540
  1.5 1.1 %copy-start.9 = (f32[128]{0:T(128)S(1)}, f32[128]{0:T(128)}, u32[]{:S(2)}) copy-start(f32[128]{0:T(128)} %param.25) | copy-start | bytes 1540
  2.6 0.7 %copy-start.6 = (s32[2,2]{1,0:T(2,128)S(1)}, s32[2,2]{1,0:T(2,128)}, u32[]{:S(2)}) copy-start(s32[2,2]{1,0:T(2,128)} %table_ref.1) | copy-start | bytes 52
  2.6 0.7 %copy-start.7 = (s32[128]{0:T(128)S(1)}, s32[128]{0:T(128)}, u32[]{:S(2)}) copy-start(s32[128]{0:T(128)} %param.15) | copy-start | bytes 1540
